TPU v7x, 512 devices: a whole 4x8x8 slice. The times are simulated.
512 devices in a mesh: row: 16 (over z, core), col: 32 (over y, x).
Axes of the slice: x: 4, y: 8, z: 8, core: 2. Of those that a mesh axis runs over, the one named last changes fastest.
Arguments:
- eigvecs: float32 [65536, 4096], P('row', 'col'), may hold values from -6 to 6
- reflectors: float32 [2, 65536, 256], P(None, ('row', 'col')), may hold values from -0.046875 to 0.046875
- tau_blocks: float32 [2, 256, 256], replicated, may hold values from -0.375 to 0.375
Outputs:
- transformed: float32 [65536, 4096], P('row', 'col')
All inputs are finite; a program needn't handle non-finite values.
Results may differ from a plain program's by a relative error of at most 0.00013.
Values sent between devices are 32-bit elements; how exact they have to be, the bound alone decides.
No kernel may reach another device: no remote copies, remote signals or barrier semaphores. Data moves between devices by JAX's collectives and lax.ppermute only.
A program may use at most 64 MiB of HBM per device.

v0:
```python
import jax
import jax.numpy as jnp
from jax import lax
from jax.sharding import PartitionSpec as P

BLOCK = 64


def project_on(factor_left, factor_right):
    return jnp.einsum(
        "rk,rc->kc",
        factor_left,
        factor_right,
        precision=lax.Precision.HIGHEST,
        preferred_element_type=jnp.float32,
    )


def multiply(factor_left, factor_right):
    return jnp.dot(
        factor_left,
        factor_right,
        precision=lax.Precision.HIGHEST,
        preferred_element_type=jnp.float32,
    )


def shape_one(drawn, panel_at, row_index, row_count):
    local_rows = jnp.arange(drawn.shape[0], dtype=jnp.int32)
    matrix_rows = local_rows // BLOCK * BLOCK * row_count + row_index * BLOCK + local_rows % BLOCK
    matrix_rows = matrix_rows[:, None]
    col_ids = jnp.arange(drawn.shape[1], dtype=jnp.int32)[None, :]
    diagonal_at = col_ids + panel_at * drawn.shape[1]
    return jnp.where(
        matrix_rows < diagonal_at,
        jnp.float32(0.0),
        jnp.where(matrix_rows == diagonal_at, jnp.float32(1.0), drawn),
    )


def shards(eigvecs, reflectors, tau_blocks):
    row_index = lax.axis_index("row")
    row_count = lax.axis_size("row")
    identity_mat = jnp.eye(tau_blocks.shape[1], dtype=jnp.float32)
    tri_one = jnp.triu(tau_blocks[0], 1) + identity_mat
    tri_two = jnp.triu(tau_blocks[1], 1) + identity_mat
    both_panels = lax.all_gather(reflectors, "col", axis=1, tiled=True)
    panel_two = shape_one(both_panels[1], 1, row_index, row_count)
    panel_one = shape_one(both_panels[0], 0, row_index, row_count)
    w_two = lax.psum(project_on(panel_two, eigvecs), "row")
    s_two = multiply(tri_two, w_two)
    after_two = eigvecs - multiply(panel_two, s_two)
    w_one = lax.psum(project_on(panel_one, after_two), "row")
    s_one = multiply(tri_one, w_one)
    return after_two - multiply(panel_one, s_one)


def solution(mesh):
    in_specs = (P("row", "col"), P(None, ("row", "col"), None), P())
    out_specs = P("row", "col")
    return jax.shard_map(shards, mesh=mesh, in_specs=in_specs, out_specs=out_specs, check_vma=False)
```

profile of v0, /device:TPU:1, one launch (start us, length us, event | category | flops | bytes accessed | tf_op | source)
XLA Modules:
  0.0 385.1 jit_solution(2996475246306338595)
XLA Ops:
  6.5 0.0 copy-start.1
  6.5 0.0 all-gather.2.cloned.1.call-start
  6.5 0.7 all-gather.2.cloned.1.call-update
  7.3 0.0 all-reduce.3.cloned.1.call-start
  7.3 111.7 %all-gather.2.cloned.1.call-done = f32[2,4096,256]{2,1,0:T(8,128)} async-done(((f32[2,128,256]{2,1,0:T(8,128)}), f32[2,4096,256]{2,1,0:T(8,128)}) %all-gather.2.cloned.1.call-update) | async-done | bytes 8388624 | tf_op jit(solution)/shard_map/all_gather | solution.py:47
  119.0 10.9 %fusion.5 = f32[256,128]{1,0:T(8,128)} fusion(f32[4096,128]{1,0:T(8,128)} %param.3, f32[2,4096,256]{2,1,0:T(8,128)} %all-gather.2.cloned.1.call-done, s32[256]{0:T(256)S(1)} %iota_add_fusion, s32[4096]{0:T(1024)S(1)} %fusion.38), kind=kOutput, calls=%fused_computation.10 | convolution fusion | flops 1614807040 | bytes 6439936 | tf_op jit(solution)/shard_map/rk,rc->kc/dot_general | solution.py:10
  129.9 0.0 all-reduce.3.cloned.1.call-update
  129.9 0.2 all-reduce.5.cloned.1.call-start
  130.2 111.6 %all-reduce.3.cloned.1.call-done = f32[256,128]{1,0:T(8,128)} async-done(((f32[256,128]{1,0:T(8,128)}), f32[256,128]{1,0:T(8,128)}) %all-reduce.3.cloned.1.call-update) | async-done | bytes 131088 | tf_op jit(solution)/shard_map/psum | solution.py:50
  241.7 0.0 copy-done.1
  241.7 1.3 fusion.24
  243.0 0.0 copy-start
  243.0 5.9 %convolution_subtract_fusion.1 = f32[4096,128]{1,0:T(8,128)S(1)} fusion(f32[4096,128]{1,0:T(8,128)} %param.3, f32[256,128]{1,0:T(8,128)S(1)} %fusion.24, f32[2,4096,256]{2,1,0:T(8,128)} %all-gather.2.cloned.1.call-done, s32[256]{0:T(256)S(1)} %iota_add_fusion, s32[4096]{0:T(1024)S(1)} %fusion.38), kind=kOutput, calls=%fused_computation.1 | convolution fusion | flops 1615331328 | bytes 8537088 | tf_op jit(solution)/shard_map/dot_general | solution.py:20
  248.9 0.0 copy-done
  248.9 8.2 %fusion.8 = f32[256,128]{1,0:T(8,128)} fusion(f32[4096,128]{1,0:T(8,128)S(1)} %convolution_subtract_fusion.1, f32[2,4096,256]{2,1,0:T(8,128)S(1)} %copy-done, s32[4096]{0:T(1024)S(1)} %fusion.38), kind=kOutput, calls=%fused_computation.11 | convolution fusion | flops 1614807040 | bytes 6438912 | tf_op jit(solution)/shard_map/rk,rc->kc/dot_general | solution.py:10
  257.1 0.0 all-reduce.5.cloned.1.call-update
  257.1 113.6 %all-reduce.5.cloned.1.call-done = f32[256,128]{1,0:T(8,128)} async-done(((f32[256,128]{1,0:T(8,128)}), f32[256,128]{1,0:T(8,128)}) %all-reduce.5.cloned.1.call-update) | async-done | bytes 131088 | tf_op jit(solution)/shard_map/psum | solution.py:53
  370.7 1.3 fusion.25
  372.0 6.5 %convolution_subtract_fusion = f32[4096,128]{1,0:T(8,128)} fusion(f32[4096,128]{1,0:T(8,128)S(1)} %convolution_subtract_fusion.1, f32[256,128]{1,0:T(8,128)S(1)} %fusion.25, f32[2,4096,256]{2,1,0:T(8,128)} %all-gather.2.cloned.1.call-done, s32[4096]{0:T(1024)S(1)} %fusion.38), kind=kOutput, calls=%fused_computation | convolution fusion | flops 1615331328 | bytes 8536064 | tf_op jit(solution)/shard_map/dot_general | solution.py:20
  (2 shorter events, 0.0 us)
Async XLA Ops:
  6.5 235.2 %copy-start.1 = (f32[2,256,256]{2,1,0:T(8,128)S(1)}, f32[2,256,256]{2,1,0:T(8,128)}, u32[]{:S(2)}) copy-start(f32[2,256,256]{2,1,0:T(8,128)} %param.5) | copy-start | bytes 1572868
  6.5 112.5 %all-gather.2.cloned.1.call-start = ((), (), s32[]{:S(2)}) async-start(), calls=%async_computation | async-start | bytes 8650752 | tf_op jit(solution)/shard_map/all_gather | solution.py:47
  7.3 234.5 %all-reduce.3.cloned.1.call-start = ((), (), s32[]{:S(2)}) async-start(), calls=%async_computation.1 | async-start | bytes 262144 | tf_op jit(solution)/shard_map/psum | solution.py:50
  129.9 240.8 %all-reduce.5.cloned.1.call-start = ((), (), s32[]{:S(2)}) async-start(), calls=%async_computation.2 | async-start | bytes 262144 | tf_op jit(solution)/shard_map/psum | solution.py:53
  243.0 5.9 %copy-start = (f32[2,4096,256]{2,1,0:T(8,128)S(1)}, f32[2,4096,256]{2,1,0:T(8,128)}, u32[]{:S(2)}) copy-start(f32[2,4096,256]{2,1,0:T(8,128)} %all-gather.2.cloned.1.call-done) | copy-start | bytes 25165828
Sparse Core Ops, SparseCore 0:
  10.5 108.4 all-gather.1
  130.1 111.6 all-reduce.2
  257.3 113.4 all-reduce.4
where the time goes:
time: 385 us
  waiting for transfers between devices  338 us (88%)
  matrix products  34 us (9%)
  between operations  13.2 us (3%)
    psum x1, waiting for transfers between devices, shards(): w_one = lax.psum(project_on(panel_one, after_two), 'row')  114 us
    all_gather x1, waiting for transfers between devices, shards(): both_panels = lax.all_gather(reflectors, 'col', axis=1, tiled=True)  112 us
    psum x1, waiting for transfers between devices, shards(): w_two = lax.psum(project_on(panel_two, eigvecs), 'row')  112 us
    dot_general x2, matrix products, project_on(): jnp.einsum('rk,rc->kc', factor_left, factor_right, precision=lax.Precisio...  19.1 us
    dot_general x4, matrix products, multiply(): jnp.dot(factor_left, factor_right, precision=lax.Precision.HIGHEST, prefe...  15 us
  transfers between devices with their start and end apart: 3, of which 3 were waited for; matrix products, arithmetic and copies ran while one was open for 0% of the time, Pallas kernels for 0%

commit v1 on v0

v1 whole, which is shorter than its diff:
```python
import jax
import jax.numpy as jnp
from jax import lax
from jax.sharding import PartitionSpec as P

BLOCK = 64


def contract(left, right, left_dim, right_dim, precision=lax.Precision.HIGHEST):
    return lax.dot_general(
        left,
        right,
        (((left_dim,), (right_dim,)), ((), ())),
        precision=precision,
        preferred_element_type=jnp.float32,
    )


def shape_own(drawn, row_index, col_index, row_count):
    panels, rows, width = drawn.shape
    local_rows = col_index * rows + jnp.arange(rows, dtype=jnp.int32)
    matrix_rows = local_rows // BLOCK * BLOCK * row_count + row_index * BLOCK + local_rows % BLOCK
    matrix_rows = matrix_rows[None, :, None]
    diagonal_at = (
        jnp.arange(panels, dtype=jnp.int32)[:, None, None] * width
        + jnp.arange(width, dtype=jnp.int32)[None, None, :]
    )
    return jnp.where(
        matrix_rows < diagonal_at,
        jnp.float32(0.0),
        jnp.where(matrix_rows == diagonal_at, jnp.float32(1.0), drawn),
    )


def sum_everywhere(partial, row_count):
    rows, width = partial.shape
    pieces = partial.reshape(row_count, rows // row_count, width)
    own = jnp.sum(lax.all_to_all(pieces, "row", 0, 0), axis=0)
    own = jnp.sum(lax.all_gather(own, "col"), axis=0)
    return lax.all_gather(own, "row", axis=0, tiled=True)


def shards(eigvecs, reflectors, tau_blocks):
    row_index = lax.axis_index("row")
    col_index = lax.axis_index("col")
    row_count = lax.axis_size("row")
    width = tau_blocks.shape[1]
    identity_mat = jnp.eye(width, dtype=jnp.float32)
    tri_one = jnp.triu(tau_blocks[0], 1) + identity_mat
    tri_two = jnp.triu(tau_blocks[1], 1) + identity_mat

    own = shape_own(reflectors, row_index, col_index, row_count)
    panels = lax.all_gather(own, "col", axis=1, tiled=True)

    gram = sum_everywhere(contract(own[0], own[1], 0, 0), row_count)
    cross = contract(tri_one, contract(gram, tri_two, 1, 0), 1, 0)

    w_two = contract(eigvecs, panels[1], 0, 0, lax.Precision.HIGH)
    w_one = contract(eigvecs, panels[0], 0, 0, lax.Precision.HIGH)
    w_both = jnp.concatenate([w_two, w_one], axis=1)
    pieces = w_both.reshape(row_count, w_both.shape[0] // row_count, 2 * width)
    w_own = jnp.sum(lax.all_to_all(pieces, "row", 0, 0), axis=0)
    s_two = contract(w_own[:, :width], tri_two, 1, 1)
    s_one = contract(w_own[:, width:], tri_one, 1, 1) - contract(w_own[:, :width], cross, 1, 1)
    s_both = lax.all_gather(jnp.concatenate([s_two, s_one], axis=1), "row", axis=0, tiled=True)

    change = contract(panels[1], s_both[:, :width], 1, 1, lax.Precision.HIGH) + contract(
        panels[0], s_both[:, width:], 1, 1, lax.Precision.HIGH
    )
    return eigvecs - change


def solution(mesh):
    in_specs = (P("row", "col"), P(None, ("row", "col"), None), P())
    out_specs = P("row", "col")
    return jax.shard_map(shards, mesh=mesh, in_specs=in_specs, out_specs=out_specs, check_vma=False)
```

time: 385 us -> 195 us (0.51)
  waiting for transfers between devices: 338 us -> 44.6 us
  blocking collectives: 0 us -> 100 us
  matrix products: 34 us -> 23.6 us
  starting transfers between devices: 0.26 us -> 8.13 us
    psum x2 -> x0, waiting for transfers between devices: 225 us -> none  [the longest x1 114 us: shards(): w_one = lax.psum(project_on(panel_one, after_two), 'row')]
    all_gather x0 -> x3, blocking collectives: none -> 76.9 us  [the longest x1 40.7 us: sum_everywhere(): own = jnp.sum(lax.all_gather(own, 'col'), axis=0)]
    all_gather x1, waiting for transfers between devices: 112 us -> 44.6 us  [shards(): panels = lax.all_gather(own, 'col', axis=1, tiled=True)]
    all_to_all x0 -> x1, blocking collectives: none -> 23.3 us  [sum_everywhere(): own = jnp.sum(lax.all_to_all(pieces, 'row', 0, 0), axis=0)]
    dot_general x6 -> x10, matrix products: 34 us -> 23.6 us  [contract(): lax.dot_general(left, right, (((left_dim,), (right_dim,)), ((), ())), pre...]
    all_to_all x0 -> x1, starting transfers between devices: none -> 8.13 us  [shards(): w_own = jnp.sum(lax.all_to_all(pieces, 'row', 0, 0), axis=0)]
  transfers between devices with their start and end apart: 3 -> 2, of which waited for: 3 -> 1; matrix products, arithmetic and copies ran while one was open for 0% -> 2% of each run, Pallas kernels for 0% -> 0%
where the time goes in v1:
time: 195 us; the launch traced here: 194 us
  blocking collectives  100 us (51%)
  waiting for transfers between devices  44.6 us (23%)
  matrix products  23.6 us (12%)
  between operations  13.5 us (7%)
  starting transfers between devices  8.13 us (4%)
  other arithmetic  2.09 us (1%)
    all_gather x1, waiting for transfers between devices, shards(): panels = lax.all_gather(own, 'col', axis=1, tiled=True)  44.6 us
    all_gather x1, blocking collectives, sum_everywhere(): own = jnp.sum(lax.all_gather(own, 'col'), axis=0)  40.7 us
    dot_general x10, matrix products, contract(): lax.dot_general(left, right, (((left_dim,), (right_dim,)), ((), ())), pre...  23.6 us
    all_to_all x1, blocking collectives, sum_everywhere(): own = jnp.sum(lax.all_to_all(pieces, 'row', 0, 0), axis=0)  23.3 us
    all_gather x1, blocking collectives, sum_everywhere(): return lax.all_gather(own, 'row', axis=0, tiled=True)  20.6 us
    all_gather x1, blocking collectives, shards(): lax.all_gather(jnp.concatenate([s_two, s_one], axis=1), 'row', axis=0, ti...  15.6 us
    all_to_all x1, starting transfers between devices, shards(): w_own = jnp.sum(lax.all_to_all(pieces, 'row', 0, 0), axis=0)  8.13 us
  transfers between devices with their start and end apart: 2, of which 1 were waited for; matrix products, arithmetic and copies ran while one was open for 2% of the time, Pallas kernels for 0%

profile of v1, /device:TPU:1, one launch (start us, length us, event | category | flops | bytes accessed | tf_op | source)
XLA Modules:
  0.0 194.1 jit_solution(17359754085532840190)
XLA Ops:
  6.5 0.0 copy-start
  6.5 0.0 all-gather.3.cloned.1.call-start
  6.5 0.1 iota_add_fusion
  6.6 1.9 select_select_fusion
  8.5 0.0 all-gather.3.cloned.1.call-update
  8.5 0.9 slice_bitcast_fusion.12
  9.5 0.1 copy.8
  9.6 1.3 fusion.12
  10.8 23.3 %all_to_all.10 = f32[16,16,256]{2,1,0:T(8,128)S(1)} all-to-all(f32[16,16,256]{2,1,0:T(8,128)S(1)} %fusion.12), channel_id=1, replica_groups=mesh['row'=16,'col'=32] {'row'}, dimensions={0} | all-to-all | bytes 524288 | tf_op jit(solution)/shard_map/all_to_all | solution.py:38
  34.2 40.7 %all-gather = f32[512,256]{1,0:T(8,128)S(1)} all-gather(f32[16,256]{1,0:T(8,128)S(1)} %reduce_sum.28), channel_id=2, replica_groups=mesh['row'=16,'col'=32] {'col'}, dimensions={0}, use_global_device_ids=true | all-gather | bytes 540672 | tf_op jit(solution)/shard_map/all_gather | solution.py:39
  74.9 44.6 %all-gather.3.cloned.1.call-done = f32[2,4096,256]{2,1,0:T(8,128)} async-done(((f32[2,128,256]{2,1,0:T(8,128)}), f32[2,4096,256]{2,1,0:T(8,128)}) %all-gather.3.cloned.1.call-update) | async-done | bytes 8388624 | tf_op jit(solution)/shard_map/all_gather | solution.py:53
  119.6 0.0 copy-done
  119.6 5.6 %fusion.4 = f32[128,256]{0,1:T(8,128)S(1)} fusion(f32[4096,128]{1,0:T(8,128)S(1)} %copy-done, f32[2,4096,256]{2,1,0:T(8,128)} %all-gather.3.cloned.1.call-done), kind=kOutput, calls=%fused_computation.7 | convolution fusion | flops 805306368 | bytes 6422528 | tf_op jit(solution)/shard_map/dot_general | solution.py:10
  125.2 0.0 copy-start.1
  125.2 5.7 %fusion.5 = f32[128,256]{0,1:T(8,128)S(1)} fusion(f32[4096,128]{1,0:T(8,128)S(1)} %copy-done, f32[2,4096,256]{2,1,0:T(8,128)} %all-gather.3.cloned.1.call-done), kind=kOutput, calls=%fused_computation.8 | convolution fusion | flops 805306368 | bytes 6422528 | tf_op jit(solution)/shard_map/dot_general | solution.py:10
  130.9 0.8 copy.7
  131.7 8.1 %all-to-all-start = ((f32[16,8,512]{2,1,0:T(8,128)}), f32[16,8,512]{2,1,0:T(8,128)S(1)}, u32[]{:S(2)}, u32[]{:S(2)}) async-start(f32[16,8,512]{2,1,0:T(8,128)} %bitcast.4), calls=%async_computation | async-start | bytes 524288 | tf_op jit(solution)/shard_map/all_to_all | solution.py:62
  139.9 20.6 %all_gather.18 = f32[256,256]{1,0:T(8,128)S(1)} all-gather(f32[16,256]{1,0:T(8,128)S(1)} %reduce_sum.29), channel_id=1, replica_groups=mesh['row'=16,'col'=32] {'row'}, dimensions={0}, use_global_device_ids=true | all-gather | bytes 278528 | tf_op jit(solution)/shard_map/all_gather | solution.py:40
  160.5 0.0 copy-done.1
  160.5 0.4 fusion.6
  160.9 0.4 fusion.8
  161.3 0.0 all-to-all-done
  161.3 0.3 fusion.9
  161.6 0.3 fusion.7
  161.9 0.3 convolution_subtract_fusion
  162.3 15.6 %all_gather.19 = f32[128,512]{1,0:T(8,128)S(1)} all-gather(f32[8,512]{1,0:T(8,128)S(1)} %pad_maximum_fusion.1), channel_id=1, replica_groups=mesh['row'=16,'col'=32] {'row'}, dimensions={0}, use_global_device_ids=true | all-gather | bytes 278528 | tf_op jit(solution)/shard_map/all_gather | solution.py:65
  177.9 4.0 %fusion.1 = f32[4096,128]{1,0:T(8,128)S(1)} fusion(f32[2,4096,256]{2,1,0:T(8,128)} %all-gather.3.cloned.1.call-done, f32[128,512]{1,0:T(8,128)S(1)} %all_gather.19), kind=kOutput, calls=%fused_computation.4 | convolution fusion | flops 805306368 | bytes 6422528 | tf_op jit(solution)/shard_map/dot_general | solution.py:10
  181.9 5.4 %fusion = f32[4096,128]{1,0:T(8,128)} fusion(f32[4096,128]{1,0:T(8,128)S(1)} %copy-done, f32[4096,128]{1,0:T(8,128)S(1)} %fusion.1, f32[2,4096,256]{2,1,0:T(8,128)} %all-gather.3.cloned.1.call-done, f32[128,512]{1,0:T(8,128)S(1)} %all_gather.19), kind=kOutput, calls=%fused_computation.1 | convolution fusion | flops 806354944 | bytes 10616832 | tf_op jit(solution)/shard_map/dot_general | solution.py:10
  (7 shorter events, 0.1 us)
Async XLA Ops:
  6.5 113.0 %copy-start = (f32[4096,128]{1,0:T(8,128)S(1)}, f32[4096,128]{1,0:T(8,128)}, u32[]{:S(2)}) copy-start(f32[4096,128]{1,0:T(8,128)} %param.3) | copy-start | bytes 6291460
  6.5 113.0 %all-gather.3.cloned.1.call-start = ((), (), s32[]{:S(2)}) async-start(), calls=%async_computation.2 | async-start | bytes 8650752 | tf_op jit(solution)/shard_map/all_gather | solution.py:53
  125.2 35.3 %copy-start.1 = (f32[2,256,256]{2,1,0:T(8,128)S(1)}, f32[2,256,256]{2,1,0:T(8,128)}, u32[]{:S(2)}) copy-start(f32[2,256,256]{2,1,0:T(8,128)} %param.5) | copy-start | bytes 1572868
  131.7 29.6 %all-to-all-start = ((f32[16,8,512]{2,1,0:T(8,128)}), f32[16,8,512]{2,1,0:T(8,128)S(1)}, u32[]{:S(2)}, u32[]{:S(2)}) async-start(f32[16,8,512]{2,1,0:T(8,128)} %bitcast.4), calls=%async_computation | async-start | bytes 524288 | tf_op jit(solution)/shard_map/all_to_all | solution.py:62
Sparse Core Ops, SparseCore 0:
  10.5 108.9 all-gather.2

commit v2 on v1

v2 whole, which is shorter than its diff:
```python
import functools

import jax
import jax.numpy as jnp
from jax import lax
from jax.experimental import pallas as pl
from jax.experimental.pallas import tpu as pltpu
from jax.sharding import PartitionSpec as P

BLOCK = 64
NX = 4
NY = 8
ROWS_A = 56
STEP_Y = 2
VMEM = 56 * 1024 * 1024


def split(value):
    high = value.astype(jnp.bfloat16)
    low = (value - high.astype(jnp.float32)).astype(jnp.bfloat16)
    return high, low


def dot(left, right):
    return jnp.dot(left, right, preferred_element_type=jnp.float32)


def shape_own(drawn, row_index, col_index, row_count):
    panels, rows, width = drawn.shape
    local_rows = col_index * rows + jnp.arange(rows, dtype=jnp.int32)
    matrix_rows = local_rows // BLOCK * BLOCK * row_count + row_index * BLOCK + local_rows % BLOCK
    matrix_rows = matrix_rows[None, :, None]
    diagonal_at = (
        jnp.arange(panels, dtype=jnp.int32)[:, None, None] * width
        + jnp.arange(width, dtype=jnp.int32)[None, None, :]
    )
    return jnp.where(
        matrix_rows < diagonal_at,
        jnp.float32(0.0),
        jnp.where(matrix_rows == diagonal_at, jnp.float32(1.0), drawn),
    )


def ring(axis_shift):
    return [(y * NX + x, y * NX + (x + axis_shift) % NX) for y in range(NY) for x in range(NX)]


GROUPS_X = [[y * NX + x for x in range(NX)] for y in range(NY)]
GROUPS_Y = [[y * NX + x for y in range(NY)] for x in range(NX)]


def spread(value, groups):
    count = len(groups[0])
    copies = jnp.broadcast_to(value[None], (count,) + value.shape)
    return lax.all_to_all(copies, "col", 0, 0, axis_index_groups=groups)


def eig_rows(eig_ref, first_y, count_y, x_at):
    parts = []
    for y in range(count_y):
        parts.append(eig_ref[pl.ds((first_y + y) * NX + x_at, 1), ROWS_A:, :])
    block = jnp.concatenate(parts, axis=0)
    return block.reshape(block.shape[0] * block.shape[1], block.shape[2])


def add_products(inner_ref, gram_ref, eig, panel):
    cols = eig.shape[1]
    width = panel.shape[1] // 2
    high, low = split(eig.T)
    parts = jnp.concatenate([high, low], axis=0)
    panel_high, panel_low = split(panel)
    both = dot(parts, panel_high)
    inner_ref[...] += both[:cols] + (both[cols:] + dot(high, panel_low))
    high = panel_high[:, width:].T
    low = panel_low[:, width:].T
    gram_ref[...] += dot(high, panel_high[:, :width]) + (
        dot(low, panel_high[:, :width]) + dot(high, panel_low[:, :width])
    )


def inner_b_kernel(x_ref, eig_ref, own_ref, left_ref, right_ref, inner_ref, gram_ref):
    @pl.when(pl.program_id(0) == 0)
    def _():
        inner_ref[...] = jnp.zeros_like(inner_ref)
        gram_ref[...] = jnp.zeros_like(gram_ref)

    x_at = x_ref[0]
    for panel_ref, shift in ((own_ref, 0), (left_ref, NX - 1), (right_ref, 1)):
        eig = eig_rows(eig_ref, 0, NY // 2, (x_at + shift) % NX)
        add_products(inner_ref, gram_ref, eig, panel_ref[...])


def inner_b(x_at, eig_blocks, own, left, right):
    blocks, block_rows, cols = eig_blocks.shape
    rows, width = own.shape
    piece = pl.BlockSpec((rows // 2, width), lambda i, x: (i, 0))
    shapes = [(cols, width), (width // 2, width // 2)]
    return pl.pallas_call(
        inner_b_kernel,
        grid_spec=pltpu.PrefetchScalarGridSpec(
            num_scalar_prefetch=1,
            grid=(2,),
            in_specs=[pl.BlockSpec((blocks // 2, block_rows, cols), lambda i, x: (i, 0, 0)), piece, piece, piece],
            out_specs=[pl.BlockSpec(shape, lambda i, x: (0, 0)) for shape in shapes],
        ),
        out_shape=[jax.ShapeDtypeStruct(shape, jnp.float32) for shape in shapes],
        compiler_params=pltpu.CompilerParams(vmem_limit_bytes=VMEM),
        cost_estimate=pl.CostEstimate(
            flops=36 * rows * cols * width, bytes_accessed=16 * rows * width, transcendentals=0
        ),
    )(x_at, eig_blocks, own, left, right)


def inner_a_kernel(
    x_ref, eig_ref, far_eig_ref, panel_ref, far_low_ref, far_high_ref, inner_start, gram_start, out_ref, inner_ref, gram_ref
):
    step = pl.program_id(0)
    x_far = (x_ref[0] + NX // 2) % NX

    @pl.when(step == 0)
    def _():
        inner_ref[...] = inner_start[...]
        gram_ref[...] = gram_start[...]
        add_products(inner_ref, gram_ref, eig_rows(far_eig_ref, 0, NY // 2, x_far), far_low_ref[...])

    @pl.when(step == 1)
    def _():
        add_products(inner_ref, gram_ref, eig_rows(far_eig_ref, 0, NY // 2, x_far), far_high_ref[...])

    eig = eig_ref[:, :ROWS_A, :]
    add_products(inner_ref, gram_ref, eig.reshape(eig.shape[0] * ROWS_A, eig.shape[2]), panel_ref[...])

    @pl.when(step == pl.num_programs(0) - 1)
    def _():
        shares, share, width = out_ref.shape
        half = gram_ref.shape[0] // 2
        out_ref[:, : share // 2, :] = inner_ref[...].reshape(shares, share // 2, width)
        gram = jnp.concatenate([gram_ref[:half, :], gram_ref[half:, :]], axis=1)
        out_ref[:, share // 2 :, :] = gram.reshape(shares, share // 2, width)


def inner_a(shares, x_at, eig_blocks, panels, far_low, far_high, inner, gram):
    blocks, block_rows, cols = eig_blocks.shape
    rows, width = panels.shape
    steps = NY // STEP_Y
    whole = lambda value: pl.BlockSpec(value.shape, lambda i, x: (0, 0))
    shape = (shares, 2 * cols // shares, width)
    return pl.pallas_call(
        inner_a_kernel,
        grid_spec=pltpu.PrefetchScalarGridSpec(
            num_scalar_prefetch=1,
            grid=(steps,),
            in_specs=[
                pl.BlockSpec((blocks // steps, block_rows, cols), lambda i, x: (i, 0, 0)),
                pl.BlockSpec((blocks // 2, block_rows, cols), lambda i, x: (jnp.minimum(i, 1), 0, 0)),
                pl.BlockSpec((rows // steps, width), lambda i, x: (i, 0)),
                whole(far_low),
                whole(far_high),
                whole(inner),
                whole(gram),
            ],
            out_specs=pl.BlockSpec(shape, lambda i, x: (0, 0, 0)),
            scratch_shapes=[pltpu.VMEM(inner.shape, jnp.float32), pltpu.VMEM(gram.shape, jnp.float32)],
        ),
        out_shape=jax.ShapeDtypeStruct(shape, jnp.float32),
        compiler_params=pltpu.CompilerParams(vmem_limit_bytes=VMEM),
        cost_estimate=pl.CostEstimate(
            flops=14 * rows * cols * width, bytes_accessed=5 * rows * width, transcendentals=0
        ),
    )(x_at, eig_blocks, eig_blocks, panels, far_low, far_high, inner, gram)


def times(left, right):
    return lax.dot_general(
        left,
        right,
        (((1,), (1,)), ((), ())),
        precision=lax.Precision.HIGHEST,
        preferred_element_type=jnp.float32,
    )


def triangle(tau):
    row = lax.broadcasted_iota(jnp.int32, tau.shape, 0)
    col = lax.broadcasted_iota(jnp.int32, tau.shape, 1)
    return jnp.where(row < col, tau, jnp.where(row == col, jnp.float32(1.0), jnp.float32(0.0)))


def update_kernel(
    x_ref, eig_ref, sums_ref, tau_ref, panel_ref, own_ref, left_ref, right_ref, far_low_ref, far_high_ref, out_ref, parts_ref
):
    cols = eig_ref.shape[2]
    width = tau_ref.shape[1]
    step = pl.program_id(0)
    half = pl.num_programs(0) // 2
    x_at = x_ref[0]

    @pl.when(step == 0)
    def _():
        own_cols = sums_ref.shape[1] // 2
        inner = sums_ref[:, :own_cols, :].reshape(cols, 2 * width)
        gram = sums_ref[:, own_cols:, :].reshape(cols, 2 * width)
        gram = jnp.concatenate([gram[:, :width], gram[:, width:]], axis=0)
        s_two = times(inner[:, :width], triangle(tau_ref[1]))
        s_one = times(inner[:, width:] - times(s_two, gram), triangle(tau_ref[0]))
        high, low = split(jnp.concatenate([s_two, s_one], axis=1).T)
        parts_ref[:, :cols] = high
        parts_ref[:, cols:] = low

    def change(panel):
        high, low = split(panel)
        both = dot(high, parts_ref[...])
        return both[:, :cols] + (both[:, cols:] + dot(low, parts_ref[:, :cols]))

    panel = panel_ref[...]
    blocks = eig_ref.shape[0]
    out_ref[:, :ROWS_A, :] = eig_ref[:, :ROWS_A, :] - change(panel).reshape(blocks, ROWS_A, cols)

    def update_rest(panel, shift):
        part = change(panel).reshape(STEP_Y, -1, cols)
        x_from = (x_at + shift) % NX
        for y in range(STEP_Y):
            at = pl.ds(y * NX + x_from, 1)
            out_ref[at, ROWS_A:, :] = eig_ref[at, ROWS_A:, :] - part[y : y + 1]

    update_rest(own_ref[...], 0)
    update_rest(left_ref[...], NX - 1)
    update_rest(right_ref[...], 1)
    update_rest(jnp.where(step < half, far_low_ref[...], far_high_ref[...]), NX // 2)


def update(x_at, eig_blocks, sums, tau, panels, own, left, right, far_low, far_high):
    blocks, block_rows, cols = eig_blocks.shape
    rows, width = panels.shape
    steps = NY // STEP_Y
    half = steps // 2
    piece_rows = own.shape[0] // steps
    piece = pl.BlockSpec((piece_rows, width), lambda i, x: (i, 0))
    block = pl.BlockSpec((blocks // steps, block_rows, cols), lambda i, x: (i, 0, 0))
    return pl.pallas_call(
        update_kernel,
        grid_spec=pltpu.PrefetchScalarGridSpec(
            num_scalar_prefetch=1,
            grid=(steps,),
            in_specs=[
                block,
                pl.BlockSpec(sums.shape, lambda i, x: (0, 0, 0)),
                pl.BlockSpec(tau.shape, lambda i, x: (0, 0, 0)),
                pl.BlockSpec((rows // steps, width), lambda i, x: (i, 0)),
                piece,
                piece,
                piece,
                pl.BlockSpec((piece_rows, width), lambda i, x: (jnp.minimum(i, half - 1), 0)),
                pl.BlockSpec((piece_rows, width), lambda i, x: (jnp.maximum(i - half, 0), 0)),
            ],
            out_specs=block,
            scratch_shapes=[pltpu.VMEM((width, 2 * cols), jnp.bfloat16)],
        ),
        out_shape=jax.ShapeDtypeStruct(eig_blocks.shape, jnp.float32),
        compiler_params=pltpu.CompilerParams(vmem_limit_bytes=VMEM),
        cost_estimate=pl.CostEstimate(
            flops=6 * blocks * block_rows * cols * width,
            bytes_accessed=4 * blocks * block_rows * (width + 2 * cols),
            transcendentals=0,
        ),
    )(x_at, eig_blocks, sums, tau, panels, own, left, right, far_low, far_high)


def shards(eigvecs, reflectors, tau_blocks):
    row_index = lax.axis_index("row")
    col_index = lax.axis_index("col")
    row_count = lax.axis_size("row")
    col_count = lax.axis_size("col")
    width = tau_blocks.shape[1]
    cols = eigvecs.shape[1]
    x_at = (col_index % NX).astype(jnp.int32)[None]
    eig_blocks = eigvecs.reshape(col_count, eigvecs.shape[0] // col_count, cols)

    own_panels = shape_own(reflectors, row_index, col_index, row_count)
    own = jnp.concatenate([own_panels[1], own_panels[0]], axis=1)

    part_a = lax.all_gather(own[:ROWS_A], "col", axis=0, tiled=True, axis_index_groups=GROUPS_X)
    part_b = spread(own[ROWS_A:], GROUPS_Y).reshape(-1, 2 * width)
    part_a, part_b = lax.optimization_barrier((part_a, part_b))
    panels_a = lax.all_gather(part_a, "col", axis=0, tiled=True, axis_index_groups=GROUPS_Y)
    left = lax.ppermute(part_b, "col", ring(1))
    right = lax.ppermute(part_b, "col", ring(-1))
    half = part_b.shape[0] // 2
    far_low = lax.ppermute(left[:half], "col", ring(1))
    far_high = lax.ppermute(right[half:], "col", ring(-1))

    inner, gram = inner_b(x_at, eig_blocks, part_b, left, right)
    shares = inner_a(row_count, x_at, eig_blocks, panels_a, far_low, far_high, inner, gram)
    share = jnp.sum(lax.all_to_all(shares, "row", 0, 0), axis=0)
    sums = lax.all_gather(share, "row")
    out = update(x_at, eig_blocks, sums, tau_blocks, panels_a, part_b, left, right, far_low, far_high)
    return out.reshape(eigvecs.shape)


def solution(mesh):
    in_specs = (P("row", "col"), P(None, ("row", "col"), None), P())
    out_specs = P("row", "col")
    return jax.shard_map(shards, mesh=mesh, in_specs=in_specs, out_specs=out_specs, check_vma=False)
```

time: 195 us -> 172 us (0.88)
  blocking collectives: 100 us -> 59.2 us
  matrix products: 23.6 us -> 0 us
  Pallas kernels: 0 us -> 22.7 us
  starting transfers between devices: 8.13 us -> 23.1 us
  waiting for transfers between devices: 44.6 us -> 50.3 us
    all_gather x3 -> x2, blocking collectives: 76.9 us -> 29.4 us  [the longest x1 17.3 us: shards(): sums = lax.all_gather(share, 'row')]
    all_gather x1, waiting for transfers between devices: 44.6 us -> 0.28 us  [shards(): lax.all_gather(part_a, 'col', axis=0, tiled=True, axis_index_groups=GROUP...]
    ppermute x0 -> x4, waiting for transfers between devices: none -> 31.8 us  [the longest x1 22.9 us: shards(): right = lax.ppermute(part_b, 'col', ring(-1))]
    dot_general x10 -> x0, matrix products: 23.6 us -> none  [contract(): lax.dot_general(left, right, (((left_dim,), (right_dim,)), ((), ())), pre...]
    pallas_call x0 -> x3, Pallas kernels: none -> 22.7 us  [the longest x1 9.14 us: update(): pl.pallas_call(update_kernel, grid_spec=pltpu.PrefetchScalarGridSpec(num_...]
    all_to_all x1, waiting for transfers between devices: 0.01 us -> 18.1 us  [spread(): return lax.all_to_all(copies, 'col', 0, 0, axis_index_groups=groups)]
    ppermute x0 -> x4, starting transfers between devices: none -> 15.4 us  [the longest x1 6.17 us: shards(): right = lax.ppermute(part_b, 'col', ring(-1))]
    all_to_all x1, blocking collectives: 23.3 us -> 29.8 us  [shards(): share = jnp.sum(lax.all_to_all(shares, 'row', 0, 0), axis=0)]
  transfers between devices with their start and end apart: 2 -> 6, of which waited for: 1 -> 5; matrix products, arithmetic and copies ran while one was open for 2% -> 0% of each run, Pallas kernels for 0% -> 3%
where the time goes in v2:
time: 172 us; the launch traced here: 171 us
  blocking collectives  59.2 us (34%)
  waiting for transfers between devices  50.3 us (29%)
  starting transfers between devices  23.1 us (13%)
  Pallas kernels  22.7 us (13%)
  between operations  13.5 us (8%)
    all_to_all x1, blocking collectives, shards(): share = jnp.sum(lax.all_to_all(shares, 'row', 0, 0), axis=0)  29.8 us
    ppermute x1, waiting for transfers between devices, shards(): right = lax.ppermute(part_b, 'col', ring(-1))  22.9 us
    all_to_all x1, waiting for transfers between devices, spread(): return lax.all_to_all(copies, 'col', 0, 0, axis_index_groups=groups)  18.1 us
    all_gather x1, blocking collectives, shards(): sums = lax.all_gather(share, 'row')  17.3 us
    all_gather x1, blocking collectives, shards(): lax.all_gather(own[:ROWS_A], 'col', axis=0, tiled=True, axis_index_groups...  12.1 us
    pallas_call x1, Pallas kernels, update(): pl.pallas_call(update_kernel, grid_spec=pltpu.PrefetchScalarGridSpec(num_...  9.14 us
    pallas_call x1, Pallas kernels, inner_a(): pl.pallas_call(inner_a_kernel, grid_spec=pltpu.PrefetchScalarGridSpec(num...  7.96 us
    all_to_all x1, starting transfers between devices, spread(): return lax.all_to_all(copies, 'col', 0, 0, axis_index_groups=groups)  7.65 us
  transfers between devices with their start and end apart: 6, of which 5 were waited for; matrix products, arithmetic and copies ran while one was open for 0% of the time, Pallas kernels for 3%

profile of v2, /device:TPU:1, one launch (start us, length us, event | category | flops | bytes accessed | tf_op | source)
XLA Modules:
  0.0 171.3 jit_solution(7784139104929643783)
XLA Ops:
  6.5 0.1 iota_add_fusion
  6.6 1.1 select_select_fusion
  7.7 1.2 broadcast_in_dim.22
  8.9 7.7 %all-to-all-start = ((f32[8,72,512]{2,1,0:T(8,128)}), f32[8,72,512]{2,1,0:T(8,128)S(1)}, u32[]{:S(2)}, u32[]{:S(2)}) async-start(f32[8,72,512]{2,1,0:T(8,128)} %broadcast_in_dim.22), calls=%async_computation | async-start | bytes 2359296 | tf_op jit(solution)/shard_map/all_to_all | solution.py:55
  16.5 0.0 all-gather.3.cloned.1.call-start
  16.6 12.1 %all_gather.12 = f32[224,512]{1,0:T(8,128)} all-gather(f32[56,512]{1,0:T(8,128)S(1)} %pad_maximum_fusion.1), channel_id=1, replica_groups={{0,1,2,3},{4,5,6,7},{8,9,10,11},{12,13,14,15},{16,17,18,19},{20,21,22,2..., dimensions={0}, use_global_device_ids=true | all-gather | bytes 573440 | tf_op jit(solution)/shard_map/all_gather | solution.py:282
  28.7 18.1 %all-to-all-done = f32[8,72,512]{2,1,0:T(8,128)S(1)} async-done(((f32[8,72,512]{2,1,0:T(8,128)}), f32[8,72,512]{2,1,0:T(8,128)S(1)}, u32[]{:S(2)}, u32[]{:S(2)}) %all-to-all-start) | async-done | bytes 1179680 | tf_op jit(solution)/shard_map/all_to_all | solution.py:55
  46.8 0.0 copy-start
  46.8 0.0 all-gather.3.cloned.1.call-update
  46.8 6.2 %collective-permute-start.2 = (f32[576,512]{1,0:T(8,128)S(1)}, f32[576,512]{1,0:T(8,128)S(1)}, u32[]{:S(2)}, u32[]{:S(2)}) collective-permute-start(f32[576,512]{1,0:T(8,128)S(1)} %bitcast.13), channel_id=1, source_target_pairs={{0,3},{1,0},{2,1},{3,2},{4,7},{5,4},{6,5},{7,6},{8,11},{9,8},{10,9... | collective-permute-start | bytes 3538952 | tf_op jit(solution)/shard_map/ppermute | solution.py:287
  53.0 1.9 %collective-permute-start = (f32[576,512]{1,0:T(8,128)S(1)}, f32[576,512]{1,0:T(8,128)S(1)}, u32[]{:S(2)}, u32[]{:S(2)}) collective-permute-start(f32[576,512]{1,0:T(8,128)S(1)} %bitcast.14), channel_id=1, source_target_pairs={{0,1},{1,2},{2,3},{3,0},{4,5},{5,6},{6,7},{7,4},{8,9},{9,10},{10,1... | collective-permute-start | bytes 3538952 | tf_op jit(solution)/shard_map/ppermute | solution.py:286
  54.9 22.9 %collective-permute-done.2.right_ref = f32[576,512]{1,0:T(8,128)S(1)} collective-permute-done((f32[576,512]{1,0:T(8,128)S(1)}, f32[576,512]{1,0:T(8,128)S(1)}, u32[]{:S(2)}, u32[]{:S(2)}) %collective-permute-start.2) | collective-permute-done | bytes 1179680 | tf_op jit(solution)/shard_map/ppermute | solution.py:287
  77.8 0.0 copy-start.1
  77.9 5.4 %collective-permute-start.3 = (f32[288,512]{1,0:T(8,128)S(1)}, f32[288,512]{1,0:T(8,128)}, u32[]{:S(2)}, u32[]{:S(2)}) collective-permute-start(f32[288,512]{1,0:T(8,128)S(1)} %slice.27), channel_id=1, source_target_pairs={{0,3},{1,0},{2,1},{3,2},{4,7},{5,4},{6,5},{7,6},{8,11},{9,8},{10,9... | collective-permute-start | bytes 1769480 | tf_op jit(solution)/shard_map/ppermute | solution.py:290
  83.3 0.0 collective-permute-done.left_ref
  83.3 0.0 copy-start.2
  83.4 0.0 copy-done
  83.4 0.0 copy-done.1
  83.4 1.9 %collective-permute-start.1 = (f32[288,512]{1,0:T(8,128)S(1)}, f32[288,512]{1,0:T(8,128)}, u32[]{:S(2)}, u32[]{:S(2)}) collective-permute-start(f32[288,512]{1,0:T(8,128)S(1)} %slice.26), channel_id=1, source_target_pairs={{0,1},{1,2},{2,3},{3,0},{4,5},{5,6},{6,7},{7,4},{8,9},{9,10},{10,1... | collective-permute-start | bytes 1769480 | tf_op jit(solution)/shard_map/ppermute | solution.py:289
  85.3 0.0 copy-done.2
  85.4 5.6 %shard_map.37 = (f32[128,512]{1,0:T(8,128)}, f32[256,256]{1,0:T(8,128)}) custom-call(s32[1]{0:T(128)} %bitcast.x_ref, f32[32,128,128]{2,1,0:T(8,128)} %bitcast.9, f32[576,512]{1,0:T(8,128)} %bitcast.15, f32[576,512]{1,0:T(8,128)} %copy-done.2, f32[576,512]{1,0:T(8,128)} %copy-done.1), custom_call_target="tpu_custom_call" | custom-call | flops 1358954496 | bytes 4718592 | tf_op jit(solution)/shard_map/pallas_call | solution.py:98
  91.0 3.7 %collective-permute-done.3.far_high_ref = f32[288,512]{1,0:T(8,128)} collective-permute-done((f32[288,512]{1,0:T(8,128)S(1)}, f32[288,512]{1,0:T(8,128)}, u32[]{:S(2)}, u32[]{:S(2)}) %collective-permute-start.3) | collective-permute-done | bytes 589856 | tf_op jit(solution)/shard_map/ppermute | solution.py:290
  94.7 5.2 %collective-permute-done.1.far_low_ref = f32[288,512]{1,0:T(8,128)} collective-permute-done((f32[288,512]{1,0:T(8,128)S(1)}, f32[288,512]{1,0:T(8,128)}, u32[]{:S(2)}, u32[]{:S(2)}) %collective-permute-start.1) | collective-permute-done | bytes 589856 | tf_op jit(solution)/shard_map/ppermute | solution.py:289
  99.9 0.3 all-gather.3.cloned.1.call-done.panel_ref
  100.2 8.0 %shard_map.38 = f32[16,16,512]{2,1,0:T(8,128)} custom-call(s32[1]{0:T(128)} %bitcast.x_ref, f32[32,128,128]{2,1,0:T(8,128)} %bitcast.10, f32[32,128,128]{2,1,0:T(8,128)} %bitcast.11, f32[1792,512]{1,0:T(8,128)} %all-gather.3.cloned.1.call-done.panel_ref, f32[288,512]{1,0:T(8,128)} %collective-permute-done.1.far_low_ref, ...), custom_call_target="tpu_custom_call" | custom-call | flops 1644167168 | bytes 4587520 | tf_op jit(solution)/shard_map/pallas_call | solution.py:148
  108.2 29.8 %all_to_all.10 = f32[16,16,512]{2,1,0:T(8,128)S(1)} all-to-all(f32[16,16,512]{2,1,0:T(8,128)} %shard_map.38), channel_id=1, replica_groups=mesh['row'=16,'col'=32] {'row'}, dimensions={0} | all-to-all | bytes 1048576 | tf_op jit(solution)/shard_map/all_to_all | solution.py:294
  138.0 17.3 %all-gather = f32[256,512]{1,0:T(8,128)} all-gather(f32[16,512]{1,0:T(8,128)S(1)} %reduce_sum.9), channel_id=2, replica_groups=mesh['row'=16,'col'=32] {'row'}, dimensions={0}, use_global_device_ids=true | all-gather | bytes 557056 | tf_op jit(solution)/shard_map/all_gather | solution.py:295
  155.3 9.1 %shard_map.39 = f32[32,128,128]{2,1,0:T(8,128)} custom-call(s32[1]{0:T(128)} %bitcast.x_ref, f32[32,128,128]{2,1,0:T(8,128)} %bitcast.12, f32[16,16,512]{2,1,0:T(8,128)} %bitcast.17, f32[2,256,256]{2,1,0:T(8,128)} %tau_ref.1, f32[1792,512]{1,0:T(8,128)} %all-gather.3.cloned.1.call-done.panel_ref, f32[576,512]{1,0:T(8,128)} %bitcast.16, ...), custom_call_target="tpu_custom_call" | custom-call | flops 1610612736 | bytes 12582912 | tf_op jit(solution)/shard_map/pallas_call | solution.py:240
  (8 shorter events, 0.2 us)
Async XLA Ops:
  8.9 37.9 %all-to-all-start = ((f32[8,72,512]{2,1,0:T(8,128)}), f32[8,72,512]{2,1,0:T(8,128)S(1)}, u32[]{:S(2)}, u32[]{:S(2)}) async-start(f32[8,72,512]{2,1,0:T(8,128)} %broadcast_in_dim.22), calls=%async_computation | async-start | bytes 2359296 | tf_op jit(solution)/shard_map/all_to_all | solution.py:55
  16.5 83.7 %all-gather.3.cloned.1.call-start = ((), (), s32[]{:S(2)}) async-start(), calls=%async_computation.2 | async-start | bytes 4128768 | tf_op jit(solution)/shard_map/all_gather | solution.py:285
  46.8 36.6 %copy-start = (f32[8,72,512]{2,1,0:T(8,128)}, f32[8,72,512]{2,1,0:T(8,128)S(1)}, u32[]{:S(2)}) copy-start(f32[8,72,512]{2,1,0:T(8,128)S(1)} %all-to-all-done) | copy-start | bytes 3538948
  46.8 31.0 %collective-permute-start.2 = (f32[576,512]{1,0:T(8,128)S(1)}, f32[576,512]{1,0:T(8,128)S(1)}, u32[]{:S(2)}, u32[]{:S(2)}) collective-permute-start(f32[576,512]{1,0:T(8,128)S(1)} %bitcast.13), channel_id=1, source_target_pairs={{0,3},{1,0},{2,1},{3,2},{4,7},{5,4},{6,5},{7,6},{8,11},{9,8},{10,9... | collective-permute-start | bytes 3538952 | tf_op jit(solution)/shard_map/ppermute | solution.py:287
  53.0 30.3 %collective-permute-start = (f32[576,512]{1,0:T(8,128)S(1)}, f32[576,512]{1,0:T(8,128)S(1)}, u32[]{:S(2)}, u32[]{:S(2)}) collective-permute-start(f32[576,512]{1,0:T(8,128)S(1)} %bitcast.14), channel_id=1, source_target_pairs={{0,1},{1,2},{2,3},{3,0},{4,5},{5,6},{6,7},{7,4},{8,9},{9,10},{10,1... | collective-permute-start | bytes 3538952 | tf_op jit(solution)/shard_map/ppermute | solution.py:286
  77.8 5.6 %copy-start.1 = (f32[576,512]{1,0:T(8,128)}, f32[576,512]{1,0:T(8,128)S(1)}, u32[]{:S(2)}) copy-start(f32[576,512]{1,0:T(8,128)S(1)} %collective-permute-done.2.right_ref) | copy-start | bytes 3538948
  77.9 16.8 %collective-permute-start.3 = (f32[288,512]{1,0:T(8,128)S(1)}, f32[288,512]{1,0:T(8,128)}, u32[]{:S(2)}, u32[]{:S(2)}) collective-permute-start(f32[288,512]{1,0:T(8,128)S(1)} %slice.27), channel_id=1, source_target_pairs={{0,3},{1,0},{2,1},{3,2},{4,7},{5,4},{6,5},{7,6},{8,11},{9,8},{10,9... | collective-permute-start | bytes 1769480 | tf_op jit(solution)/shard_map/ppermute | solution.py:290
  83.3 2.0 %copy-start.2 = (f32[576,512]{1,0:T(8,128)}, f32[576,512]{1,0:T(8,128)S(1)}, u32[]{:S(2)}) copy-start(f32[576,512]{1,0:T(8,128)S(1)} %collective-permute-done.left_ref) | copy-start | bytes 3538948
  83.4 16.5 %collective-permute-start.1 = (f32[288,512]{1,0:T(8,128)S(1)}, f32[288,512]{1,0:T(8,128)}, u32[]{:S(2)}, u32[]{:S(2)}) collective-permute-start(f32[288,512]{1,0:T(8,128)S(1)} %slice.26), channel_id=1, source_target_pairs={{0,1},{1,2},{2,3},{3,0},{4,5},{5,6},{6,7},{7,4},{8,9},{9,10},{10,1... | collective-permute-start | bytes 1769480 | tf_op jit(solution)/shard_map/ppermute | solution.py:289
Sparse Core Ops, SparseCore 0:
  47.0 53.2 all-gather.2

commit v3 on v1

v3 whole, which is shorter than its diff:
```python
import functools

import jax
import jax.numpy as jnp
from jax import lax
from jax.experimental import pallas as pl
from jax.experimental.pallas import tpu as pltpu
from jax.sharding import PartitionSpec as P

BLOCK = 64
NX = 4
NY = 8
VMEM = 60 * 1024 * 1024


def split(value):
    high = value.astype(jnp.bfloat16)
    low = (value - high.astype(jnp.float32)).astype(jnp.bfloat16)
    return high, low


def dot(left, right):
    return jnp.dot(left, right, preferred_element_type=jnp.float32)


def shape_own(drawn, row_index, col_index, row_count):
    panels, rows, width = drawn.shape
    local_rows = col_index * rows + jnp.arange(rows, dtype=jnp.int32)
    matrix_rows = local_rows // BLOCK * BLOCK * row_count + row_index * BLOCK + local_rows % BLOCK
    matrix_rows = matrix_rows[None, :, None]
    diagonal_at = (
        jnp.arange(panels, dtype=jnp.int32)[:, None, None] * width
        + jnp.arange(width, dtype=jnp.int32)[None, None, :]
    )
    return jnp.where(
        matrix_rows < diagonal_at,
        jnp.float32(0.0),
        jnp.where(matrix_rows == diagonal_at, jnp.float32(1.0), drawn),
    )


def move_x(value, shift):
    pairs = [(y * NX + x, y * NX + (x + shift) % NX) for y in range(NY) for x in range(NX)]
    return lax.ppermute(value, "col", pairs)


def move_y(value, shift):
    pairs = [(y * NX + x, (y + shift) % NY * NX + x) for y in range(NY) for x in range(NX)]
    return lax.ppermute(value, "col", pairs)


GROUPS_X = [[y * NX + x for x in range(NX)] for y in range(NY)]
GROUPS_Y = [[y * NX + x for y in range(NY)] for x in range(NX)]


def spread(value, groups):
    count = len(groups[0])
    copies = jnp.broadcast_to(value[None], (count,) + value.shape)
    return lax.all_to_all(copies, "col", 0, 0, axis_index_groups=groups)


OWN = [("a", 0, 0, NX), ("b", 0, 0, NY)]
NEAR = [("a", -1, 0, NX), ("a", 1, 0, NX), ("a", -2, 0, NX), ("a", 2, 0, NX), ("b", -1, 0, NY), ("b", 1, 0, NY)]
FAR = [("a", -3, 0, NX), ("a", 3, 0, NX), ("b", NX // 2, 0, NY), ("a", NY // 2, 0, NX)]


def place(piece, at):
    kind, shift, first, _ = piece
    if kind == "a":
        return (at[0] + shift + NY) % NY, first
    return first, (at[1] + shift + NX) % NX


def block_shape(piece):
    kind, _, _, count = piece
    return (1, count) if kind == "a" else (count, 1)


def add_products(inner_ref, gram_ref, eig, panel):
    cols = eig.shape[1]
    width = panel.shape[1] // 2
    high, low = split(eig.T)
    parts = jnp.concatenate([high, low], axis=0)
    panel_high, panel_low = split(panel)
    both = dot(parts, panel_high)
    inner_ref[...] += both[:cols] + (both[cols:] + dot(high, panel_low))
    high = panel_high[:, width:].T
    low = panel_low[:, width:].T
    gram_ref[...] += dot(high, panel_high[:, :width]) + (
        dot(low, panel_high[:, :width]) + dot(high, panel_low[:, :width])
    )


def inner_kernel(count, first, last, at_ref, *refs):
    eigs, panels, refs = refs[:count], refs[count : 2 * count], refs[2 * count :]
    if first:
        starts = None
    else:
        starts, refs = refs[:2], refs[2:]
    outs, (inner_ref, gram_ref) = refs[:-2], refs[-2:]
    inner_ref[...] = jnp.zeros_like(inner_ref) if first else starts[0][...]
    gram_ref[...] = jnp.zeros_like(gram_ref) if first else starts[1][...]
    for eig_ref, panel_ref in zip(eigs, panels):
        add_products(inner_ref, gram_ref, eig_ref[...].reshape(panel_ref.shape[0], -1), panel_ref[...])
    if not last:
        outs[0][...] = inner_ref[...]
        outs[1][...] = gram_ref[...]
        return
    (out_ref,) = outs
    shares, share, width = out_ref.shape
    half = gram_ref.shape[0] // 2
    out_ref[:, : share // 2, :] = inner_ref[...].reshape(shares, share // 2, width)
    gram = jnp.concatenate([gram_ref[:half, :], gram_ref[half:, :]], axis=1)
    out_ref[:, share // 2 :, :] = gram.reshape(shares, share // 2, width)


def inner_products(at, eigs, pieces, panels, starts, shares):
    _, _, _, rows, cols = eigs.shape
    width = panels[0].shape[1]
    total = sum(panel.shape[0] for panel in panels)
    state = [(cols, width), (width // 2, width // 2)]
    outs = [(shares, 2 * cols // shares, width)] if shares else state

    def eig_spec(piece):
        half = 0 if piece[0] == "a" else 1
        shape = block_shape(piece)

        def index(i, at_ref):
            y, x = place(piece, (at_ref[0], at_ref[1]))
            return y // shape[0], x // shape[1], half, 0, 0

        return pl.BlockSpec(shape + (1, rows, cols), index)

    def whole(shape):
        return pl.BlockSpec(shape, lambda i, at_ref: (0,) * len(shape))

    return pl.pallas_call(
        functools.partial(inner_kernel, len(pieces), starts is None, bool(shares)),
        grid_spec=pltpu.PrefetchScalarGridSpec(
            num_scalar_prefetch=1,
            grid=(1,),
            in_specs=[eig_spec(piece) for piece in pieces]
            + [whole(panel.shape) for panel in panels]
            + ([] if starts is None else [whole(shape) for shape in state]),
            out_specs=[whole(shape) for shape in outs],
            scratch_shapes=[pltpu.VMEM(shape, jnp.float32) for shape in state],
        ),
        out_shape=[jax.ShapeDtypeStruct(shape, jnp.float32) for shape in outs],
        compiler_params=pltpu.CompilerParams(vmem_limit_bytes=VMEM),
        cost_estimate=pl.CostEstimate(
            flops=12 * total * cols * width, bytes_accessed=4 * total * (width + cols), transcendentals=0
        ),
    )(at, *[eigs] * len(pieces), *panels, *([] if starts is None else starts))


def times(left, right):
    return lax.dot_general(
        left,
        right,
        (((1,), (1,)), ((), ())),
        precision=lax.Precision.HIGHEST,
        preferred_element_type=jnp.float32,
    )


def triangle(tau):
    row = lax.broadcasted_iota(jnp.int32, tau.shape, 0)
    col = lax.broadcasted_iota(jnp.int32, tau.shape, 1)
    return jnp.where(row < col, tau, jnp.where(row == col, jnp.float32(1.0), jnp.float32(0.0)))


def update_kernel(pieces, at_ref, sums_ref, tau_ref, eig_ref, *refs):
    count = len(pieces)
    panels, out_ref = refs[:count], refs[count]
    parts_ref, panel_buf, eig_buf, panel_sems, eig_sems, out_sems = refs[count + 1 :]
    rows, cols = eig_ref.shape[3:]
    width = tau_ref.shape[1]

    loads, stores, spans, first = [], [], [], 0
    for n, piece in enumerate(pieces):
        size = panels[n].shape[0]
        y, x = place(piece, (at_ref[0], at_ref[1]))
        shape = block_shape(piece)
        at = (pl.ds(y, shape[0]), pl.ds(x, shape[1]), 0 if piece[0] == "a" else 1)
        span = pl.ds(first // rows, size // rows)
        local = eig_buf.at[span].reshape(shape + (rows, cols))
        loads.append(
            (
                pltpu.make_async_copy(panels[n], panel_buf.at[pl.ds(first, size)], panel_sems.at[n]),
                pltpu.make_async_copy(eig_ref.at[at], local, eig_sems.at[n]),
            )
        )
        stores.append(pltpu.make_async_copy(local, out_ref.at[at], out_sems.at[n]))
        spans.append((first, size))
        first += size
    for load in loads:
        for copy in load:
            copy.start()

    own_cols = sums_ref.shape[1] // 2
    inner = sums_ref[:, :own_cols, :].reshape(cols, 2 * width)
    gram = sums_ref[:, own_cols:, :].reshape(cols, 2 * width)
    gram = jnp.concatenate([gram[:, :width], gram[:, width:]], axis=0)
    s_two = times(inner[:, :width], triangle(tau_ref[1]))
    s_one = times(inner[:, width:] - times(s_two, gram), triangle(tau_ref[0]))
    high, low = split(jnp.concatenate([s_two, s_one], axis=1).T)
    parts_ref[:, :cols] = high
    parts_ref[:, cols:] = low

    for load, store, (first, size) in zip(loads, stores, spans):
        for copy in load:
            copy.wait()
        high, low = split(panel_buf[first : first + size, :])
        both = dot(high, parts_ref[...])
        change = both[:, :cols] + (both[:, cols:] + dot(low, parts_ref[:, :cols]))
        span = slice(first // rows, (first + size) // rows)
        eig_buf[span] = eig_buf[span] - change.reshape(size // rows, rows, cols)
        store.start()
    for store in stores:
        store.wait()


def update(at, eigs, sums, tau, pieces, panels):
    rows, cols = eigs.shape[3:]
    width = panels[0].shape[1]
    total = sum(panel.shape[0] for panel in panels)
    anywhere = pl.BlockSpec(memory_space=pl.ANY)
    return pl.pallas_call(
        functools.partial(update_kernel, pieces),
        grid_spec=pltpu.PrefetchScalarGridSpec(
            num_scalar_prefetch=1,
            grid=(1,),
            in_specs=[
                pl.BlockSpec(sums.shape, lambda i, at_ref: (0, 0, 0)),
                pl.BlockSpec(tau.shape, lambda i, at_ref: (0, 0, 0)),
                anywhere,
            ]
            + [anywhere] * len(panels),
            out_specs=anywhere,
            scratch_shapes=[
                pltpu.VMEM((width, 2 * cols), jnp.bfloat16),
                pltpu.VMEM((total, width), jnp.float32),
                pltpu.VMEM((total // rows, rows, cols), jnp.float32),
            ]
            + [pltpu.SemaphoreType.DMA((len(pieces),))] * 3,
        ),
        out_shape=jax.ShapeDtypeStruct(eigs.shape, jnp.float32),
        compiler_params=pltpu.CompilerParams(vmem_limit_bytes=VMEM),
        cost_estimate=pl.CostEstimate(
            flops=6 * total * cols * width, bytes_accessed=4 * total * (width + 2 * cols), transcendentals=0
        ),
    )(at, sums, tau, eigs, *panels)


def shards(eigvecs, reflectors, tau_blocks):
    row_index = lax.axis_index("row")
    col_index = lax.axis_index("col")
    row_count = lax.axis_size("row")
    cols = eigvecs.shape[1]
    width = 2 * tau_blocks.shape[1]
    half = reflectors.shape[1] // 2
    at = jnp.stack([col_index // NX, col_index % NX]).astype(jnp.int32)
    eigs = eigvecs.reshape(NY, NX, 2, half, cols)

    own = shape_own(reflectors, row_index, col_index, row_count)
    own = jnp.concatenate([own[1], own[0]], axis=1)

    own_a = lax.all_gather(own[:half], "col", axis=0, tiled=True, axis_index_groups=GROUPS_X)
    own_b = spread(own[half:], GROUPS_Y).reshape(-1, width)
    own_b, _ = lax.optimization_barrier((own_b, own_a))
    up, down = [own_a], [own_a]
    for _ in range(NY // 2 - 1):
        up.append(move_y(up[-1], 1))
        down.append(move_y(down[-1], -1))
    left, right = move_x(own_b, 1), move_x(own_b, -1)
    far_b = move_x(left, 1)
    far_a = move_y(up[-1], 1)

    near = [up[1], down[1], up[2], down[2], left, right]
    far = [up[3], down[3], far_b, far_a]
    state = inner_products(at, eigs, OWN, [own_a, own_b], None, 0)
    state = inner_products(at, eigs, NEAR, near, state, 0)
    (shares,) = inner_products(at, eigs, FAR, far, state, row_count)
    share = jnp.sum(lax.all_to_all(shares, "row", 0, 0), axis=0)
    sums = lax.all_gather(share, "row")

    out = update(at, eigs, sums, tau_blocks, OWN + NEAR + FAR, [own_a, own_b] + near + far)
    return out.reshape(eigvecs.shape)


def solution(mesh):
    in_specs = (P("row", "col"), P(None, ("row", "col"), None), P())
    out_specs = P("row", "col")
    return jax.shard_map(shards, mesh=mesh, in_specs=in_specs, out_specs=out_specs, check_vma=False)
```

time: 195 us -> 154 us (0.79)
  blocking collectives: 100 us -> 59.5 us
  starting transfers between devices: 8.13 us -> 38.3 us
  matrix products: 23.6 us -> 0 us
  Pallas kernels: 0 us -> 23.6 us
  waiting for transfers between devices: 44.6 us -> 29.1 us
  between operations: 13.5 us -> 0.16 us
    all_gather x3 -> x2, blocking collectives: 76.9 us -> 29 us  [the longest x1 17.3 us: shards(): sums = lax.all_gather(share, 'row')]
    all_gather x1 -> x0, waiting for transfers between devices: 44.6 us -> none  [shards(): panels = lax.all_gather(own, 'col', axis=1, tiled=True)]
    ppermute x0 -> x10, starting transfers between devices: none -> 30.6 us  [the longest x7 19 us: move_y(): return lax.ppermute(value, 'col', pairs)]
    dot_general x10 -> x0, matrix products: 23.6 us -> none  [contract(): lax.dot_general(left, right, (((left_dim,), (right_dim,)), ((), ())), pre...]
    pallas_call x0 -> x4, Pallas kernels: none -> 23.6 us  [the longest x3 14.8 us: inner_products(): pl.pallas_call(functools.partial(inner_kernel, len(pieces), starts is Non...]
    ppermute x0 -> x10, waiting for transfers between devices: none -> 16.6 us  [the longest x7 11.8 us: move_y(): return lax.ppermute(value, 'col', pairs)]
    all_to_all x1, waiting for transfers between devices: 0.01 us -> 12.4 us  [spread(): return lax.all_to_all(copies, 'col', 0, 0, axis_index_groups=groups)]
    all_to_all x1, blocking collectives: 23.3 us -> 30.6 us  [shards(): share = jnp.sum(lax.all_to_all(shares, 'row', 0, 0), axis=0)]
  transfers between devices with their start and end apart: 2 -> 11, of which waited for: 1 -> 9; matrix products, arithmetic and copies ran while one was open for 2% -> 0% of each run, Pallas kernels for 0% -> 6%
where the time goes in v3:
time: 154 us
  blocking collectives  59.5 us (39%)
  starting transfers between devices  38.3 us (25%)
  waiting for transfers between devices  29.1 us (19%)
  Pallas kernels  23.6 us (15%)
  other arithmetic  1.84 us (1%)
    all_to_all x1, blocking collectives, shards(): share = jnp.sum(lax.all_to_all(shares, 'row', 0, 0), axis=0)  30.6 us
    ppermute x7, starting transfers between devices, move_y(): return lax.ppermute(value, 'col', pairs)  19 us
    all_gather x1, blocking collectives, shards(): sums = lax.all_gather(share, 'row')  17.3 us
    pallas_call x3, Pallas kernels, inner_products(): pl.pallas_call(functools.partial(inner_kernel, len(pieces), starts is Non...  14.8 us
    all_to_all x1, waiting for transfers between devices, spread(): return lax.all_to_all(copies, 'col', 0, 0, axis_index_groups=groups)  12.4 us
    ppermute x7, waiting for transfers between devices, move_y(): return lax.ppermute(value, 'col', pairs)  11.8 us
    all_gather x1, blocking collectives, shards(): lax.all_gather(own[:half], 'col', axis=0, tiled=True, axis_index_groups=G...  11.7 us
    ppermute x3, starting transfers between devices, move_x(): return lax.ppermute(value, 'col', pairs)  11.6 us
  transfers between devices with their start and end apart: 11, of which 9 were waited for; matrix products, arithmetic and copies ran while one was open for 0% of the time, Pallas kernels for 6%

profile of v3, /device:TPU:1, one launch (start us, length us, event | category | flops | bytes accessed | tf_op | source)
XLA Modules:
  0.0 153.7 jit_solution(13871904715473535156)
XLA Ops:
  0.0 0.1 iota_add_fusion
  0.1 1.1 select_select_fusion
  1.2 1.1 broadcast_in_dim.18
  2.3 7.7 %all-to-all-start = ((f32[8,64,512]{2,1,0:T(8,128)}), f32[8,64,512]{2,1,0:T(8,128)S(1)}, u32[]{:S(2)}, u32[]{:S(2)}) async-start(f32[8,64,512]{2,1,0:T(8,128)} %broadcast_in_dim.18), calls=%async_computation | async-start | bytes 2097152 | tf_op jit(solution)/shard_map/all_to_all | solution.py:59
  10.0 11.7 %all_gather.9.refs_2_.refs_0_ = f32[256,512]{1,0:T(8,128)S(1)} all-gather(f32[64,512]{1,0:T(8,128)S(1)} %get-tuple-element.16), channel_id=1, replica_groups={{0,1,2,3},{4,5,6,7},{8,9,10,11},{12,13,14,15},{16,17,18,19},{20,21,22,2..., dimensions={0}, use_global_device_ids=true | all-gather | bytes 655360 | tf_op jit(solution)/shard_map/all_gather | solution.py:268
  21.6 3.3 %collective-permute-start = (f32[256,512]{1,0:T(8,128)S(1)}, f32[256,512]{1,0:T(8,128)S(1)}, u32[]{:S(2)}, u32[]{:S(2)}) collective-permute-start(f32[256,512]{1,0:T(8,128)S(1)} %all_gather.9.refs_2_.refs_0_), channel_id=1, source_target_pairs={{0,4},{1,5},{2,6},{3,7},{4,8},{5,9},{6,10},{7,11},{8,12},{9,13},{1... | collective-permute-start | bytes 1572872 | tf_op jit(solution)/shard_map/ppermute | solution.py:49
  24.9 12.4 %all-to-all-done = f32[8,64,512]{2,1,0:T(8,128)S(1)} async-done(((f32[8,64,512]{2,1,0:T(8,128)}), f32[8,64,512]{2,1,0:T(8,128)S(1)}, u32[]{:S(2)}, u32[]{:S(2)}) %all-to-all-start) | async-done | bytes 1048608 | tf_op jit(solution)/shard_map/all_to_all | solution.py:59
  37.4 4.9 %collective-permute-start.6 = (f32[512,512]{1,0:T(8,128)S(1)}, f32[512,512]{1,0:T(8,128)S(1)}, u32[]{:S(2)}, u32[]{:S(2)}) collective-permute-start(f32[512,512]{1,0:T(8,128)S(1)} %bitcast.23), channel_id=1, source_target_pairs={{0,1},{1,2},{2,3},{3,0},{4,5},{5,6},{6,7},{7,4},{8,9},{9,10},{10,1... | collective-permute-start | bytes 3145736 | tf_op jit(solution)/shard_map/ppermute | solution.py:44
  42.3 1.9 %collective-permute-start.3 = (f32[256,512]{1,0:T(8,128)S(1)}, f32[256,512]{1,0:T(8,128)S(1)}, u32[]{:S(2)}, u32[]{:S(2)}) collective-permute-start(f32[256,512]{1,0:T(8,128)S(1)} %all_gather.9.refs_2_.refs_0_), channel_id=1, source_target_pairs={{0,28},{1,29},{2,30},{3,31},{4,0},{5,1},{6,2},{7,3},{8,4},{9,5},{1... | collective-permute-start | bytes 1572872 | tf_op jit(solution)/shard_map/ppermute | solution.py:49
  44.2 2.5 %collective-permute-done.refs_6_.refs_2_ = f32[256,512]{1,0:T(8,128)S(1)} collective-permute-done((f32[256,512]{1,0:T(8,128)S(1)}, f32[256,512]{1,0:T(8,128)S(1)}, u32[]{:S(2)}, u32[]{:S(2)}) %collective-permute-start) | collective-permute-done | bytes 524320 | tf_op jit(solution)/shard_map/ppermute | solution.py:49
  46.7 1.9 %collective-permute-start.1 = (f32[256,512]{1,0:T(8,128)S(1)}, f32[256,512]{1,0:T(8,128)S(1)}, u32[]{:S(2)}, u32[]{:S(2)}) collective-permute-start(f32[256,512]{1,0:T(8,128)S(1)} %collective-permute-done.refs_6_.refs_2_), channel_id=1, source_target_pairs={{0,4},{1,5},{2,6},{3,7},{4,8},{5,9},{6,10},{7,11},{8,12},{9,13},{1... | collective-permute-start | bytes 1572872 | tf_op jit(solution)/shard_map/ppermute | solution.py:49
  48.6 4.4 %collective-permute-start.9 = (f32[512,512]{1,0:T(8,128)S(1)}, f32[512,512]{1,0:T(8,128)}, u32[]{:S(2)}, u32[]{:S(2)}) collective-permute-start(f32[512,512]{1,0:T(8,128)S(1)} %bitcast.24), channel_id=1, source_target_pairs={{0,3},{1,0},{2,1},{3,2},{4,7},{5,4},{6,5},{7,6},{8,11},{9,8},{10,9... | collective-permute-start | bytes 3145736 | tf_op jit(solution)/shard_map/ppermute | solution.py:44
  53.1 3.7 %collective-permute-done.3.refs_7_.refs_3_ = f32[256,512]{1,0:T(8,128)S(1)} collective-permute-done((f32[256,512]{1,0:T(8,128)S(1)}, f32[256,512]{1,0:T(8,128)S(1)}, u32[]{:S(2)}, u32[]{:S(2)}) %collective-permute-start.3) | collective-permute-done | bytes 524320 | tf_op jit(solution)/shard_map/ppermute | solution.py:49
  56.7 3.3 %collective-permute-start.4 = (f32[256,512]{1,0:T(8,128)S(1)}, f32[256,512]{1,0:T(8,128)}, u32[]{:S(2)}, u32[]{:S(2)}) collective-permute-start(f32[256,512]{1,0:T(8,128)S(1)} %collective-permute-done.3.refs_7_.refs_3_), channel_id=1, source_target_pairs={{0,28},{1,29},{2,30},{3,31},{4,0},{5,1},{6,2},{7,3},{8,4},{9,5},{1... | collective-permute-start | bytes 1572872 | tf_op jit(solution)/shard_map/ppermute | solution.py:49
  60.1 1.7 %collective-permute-done.1.refs_8_.refs_4_ = f32[256,512]{1,0:T(8,128)S(1)} collective-permute-done((f32[256,512]{1,0:T(8,128)S(1)}, f32[256,512]{1,0:T(8,128)S(1)}, u32[]{:S(2)}, u32[]{:S(2)}) %collective-permute-start.1) | collective-permute-done | bytes 524320 | tf_op jit(solution)/shard_map/ppermute | solution.py:49
  61.8 1.9 %collective-permute-start.2 = (f32[256,512]{1,0:T(8,128)S(1)}, f32[256,512]{1,0:T(8,128)}, u32[]{:S(2)}, u32[]{:S(2)}) collective-permute-start(f32[256,512]{1,0:T(8,128)S(1)} %collective-permute-done.1.refs_8_.refs_4_), channel_id=1, source_target_pairs={{0,4},{1,5},{2,6},{3,7},{4,8},{5,9},{6,10},{7,11},{8,12},{9,13},{1... | collective-permute-start | bytes 1572872 | tf_op jit(solution)/shard_map/ppermute | solution.py:49
  63.7 2.2 %collective-permute-done.6.refs_10_.refs_6_ = f32[512,512]{1,0:T(8,128)S(1)} collective-permute-done((f32[512,512]{1,0:T(8,128)S(1)}, f32[512,512]{1,0:T(8,128)S(1)}, u32[]{:S(2)}, u32[]{:S(2)}) %collective-permute-start.6) | collective-permute-done | bytes 1048608 | tf_op jit(solution)/shard_map/ppermute | solution.py:44
  65.9 2.3 %collective-permute-start.7 = (f32[512,512]{1,0:T(8,128)S(1)}, f32[512,512]{1,0:T(8,128)}, u32[]{:S(2)}, u32[]{:S(2)}) collective-permute-start(f32[512,512]{1,0:T(8,128)S(1)} %collective-permute-done.6.refs_10_.refs_6_), channel_id=1, source_target_pairs={{0,1},{1,2},{2,3},{3,0},{4,5},{5,6},{6,7},{7,4},{8,9},{9,10},{10,1... | collective-permute-start | bytes 3145736 | tf_op jit(solution)/shard_map/ppermute | solution.py:44
  68.3 2.1 %collective-permute-done.4.refs_9_.refs_5_ = f32[256,512]{1,0:T(8,128)} collective-permute-done((f32[256,512]{1,0:T(8,128)S(1)}, f32[256,512]{1,0:T(8,128)}, u32[]{:S(2)}, u32[]{:S(2)}) %collective-permute-start.4) | collective-permute-done | bytes 524320 | tf_op jit(solution)/shard_map/ppermute | solution.py:49
  70.4 4.8 %collective-permute-start.5 = (f32[256,512]{1,0:T(8,128)}, f32[256,512]{1,0:T(8,128)}, u32[]{:S(2)}, u32[]{:S(2)}) collective-permute-start(f32[256,512]{1,0:T(8,128)} %collective-permute-done.4.refs_9_.refs_5_), channel_id=1, source_target_pairs={{0,28},{1,29},{2,30},{3,31},{4,0},{5,1},{6,2},{7,3},{8,4},{9,5},{1... | collective-permute-start | bytes 1572872 | tf_op jit(solution)/shard_map/ppermute | solution.py:49
  75.1 0.9 collective-permute-done.2.refs_4_.refs_8_
  76.0 1.9 %collective-permute-start.8 = (f32[256,512]{1,0:T(8,128)}, f32[256,512]{1,0:T(8,128)}, u32[]{:S(2)}, u32[]{:S(2)}) collective-permute-start(f32[256,512]{1,0:T(8,128)} %collective-permute-done.2.refs_4_.refs_8_), channel_id=1, source_target_pairs={{0,4},{1,5},{2,6},{3,7},{4,8},{5,9},{6,10},{7,11},{8,12},{9,13},{1... | collective-permute-start | bytes 1572872 | tf_op jit(solution)/shard_map/ppermute | solution.py:49
  78.0 0.6 pad_add_fusion.at_ref
  78.6 3.8 %shard_map.37 = (f32[128,512]{1,0:T(8,128)}, f32[256,256]{1,0:T(8,128)}) custom-call(s32[2]{0:T(128)} %pad_add_fusion.at_ref, f32[8,4,2,64,128]{4,3,2,1,0:T(8,128)} %bitcast.10, f32[8,4,2,64,128]{4,3,2,1,0:T(8,128)} %bitcast.11, f32[256,512]{1,0:T(8,128)} %copy-done.1, f32[512,512]{1,0:T(8,128)} %bitcast.25), custom_call_target="tpu_custom_call" | custom-call | flops 603979776 | bytes 1966080 | tf_op jit(solution)/shard_map/pallas_call | solution.py:137
  82.4 0.0 collective-permute-done.9.refs_11_.refs_7_
  82.4 6.1 %shard_map.38 = (f32[128,512]{1,0:T(8,128)}, f32[256,256]{1,0:T(8,128)}) custom-call(s32[2]{0:T(128)} %pad_add_fusion.at_ref, f32[8,4,2,64,128]{4,3,2,1,0:T(8,128)} %bitcast.12, f32[8,4,2,64,128]{4,3,2,1,0:T(8,128)} %bitcast.13, f32[8,4,2,64,128]{4,3,2,1,0:T(8,128)} %bitcast.14, f32[8,4,2,64,128]{4,3,2,1,0:T(8,128)} %bitcast.15, ...), custom_call_target="tpu_custom_call" | custom-call | flops 1610612736 | bytes 5242880 | tf_op jit(solution)/shard_map/pallas_call | solution.py:137
  88.6 1.0 collective-permute-done.8.refs_7_.refs_11_
  89.5 2.6 %collective-permute-done.7.refs_6_.refs_10_ = f32[512,512]{1,0:T(8,128)} collective-permute-done((f32[512,512]{1,0:T(8,128)S(1)}, f32[512,512]{1,0:T(8,128)}, u32[]{:S(2)}, u32[]{:S(2)}) %collective-permute-start.7) | collective-permute-done | bytes 1048608 | tf_op jit(solution)/shard_map/ppermute | solution.py:44
  92.1 4.8 %shard_map.39 = f32[16,16,512]{2,1,0:T(8,128)} custom-call(s32[2]{0:T(128)} %pad_add_fusion.at_ref, f32[8,4,2,64,128]{4,3,2,1,0:T(8,128)} %bitcast.18, f32[8,4,2,64,128]{4,3,2,1,0:T(8,128)} %bitcast.19, f32[8,4,2,64,128]{4,3,2,1,0:T(8,128)} %bitcast.20, f32[8,4,2,64,128]{4,3,2,1,0:T(8,128)} %bitcast.21, f32[256,512]{1,0:T(8,128)} %collective-permute-done.2.refs_4_.refs_8_, ...), custom_call_target="tpu_custom_call" | custom-call | flops 1006632960 | bytes 3276800 | tf_op jit(solution)/shard_map/pallas_call | solution.py:137
  96.9 30.6 %all_to_all.10 = f32[16,16,512]{2,1,0:T(8,128)S(1)} all-to-all(f32[16,16,512]{2,1,0:T(8,128)} %shard_map.39), channel_id=1, replica_groups=mesh['row'=16,'col'=32] {'row'}, dimensions={0} | all-to-all | bytes 1048576 | tf_op jit(solution)/shard_map/all_to_all | solution.py:284
  127.5 17.3 %all-gather = f32[256,512]{1,0:T(8,128)} all-gather(f32[16,512]{1,0:T(8,128)S(1)} %reduce_sum.9), channel_id=2, replica_groups=mesh['row'=16,'col'=32] {'row'}, dimensions={0}, use_global_device_ids=true | all-gather | bytes 557056 | tf_op jit(solution)/shard_map/all_gather | solution.py:285
  144.8 8.8 %shard_map.40 = f32[8,4,2,64,128]{4,3,2,1,0:T(8,128)} custom-call(s32[2]{0:T(128)} %pad_add_fusion.at_ref, f32[16,16,512]{2,1,0:T(8,128)} %bitcast.27, f32[2,256,256]{2,1,0:T(8,128)} %tau_ref.1, f32[8,4,2,64,128]{4,3,2,1,0:T(8,128)} %bitcast.22, f32[256,512]{1,0:T(8,128)} %copy-done.1, f32[512,512]{1,0:T(8,128)} %bitcast.26, f32[256,512]{1,0:T(8,128)} %copy-done.3, ...), custom_call_target="tpu_custom_call" | custom-call | flops 1610612736 | bytes 12582912 | tf_op jit(solution)/shard_map/pallas_call | solution.py:228
  (18 shorter events, 0.1 us)
Async XLA Ops:
  2.3 35.1 %all-to-all-start = ((f32[8,64,512]{2,1,0:T(8,128)}), f32[8,64,512]{2,1,0:T(8,128)S(1)}, u32[]{:S(2)}, u32[]{:S(2)}) async-start(f32[8,64,512]{2,1,0:T(8,128)} %broadcast_in_dim.18), calls=%async_computation | async-start | bytes 2097152 | tf_op jit(solution)/shard_map/all_to_all | solution.py:59
  21.6 57.0 %copy-start.1 = (f32[256,512]{1,0:T(8,128)}, f32[256,512]{1,0:T(8,128)S(1)}, u32[]{:S(2)}) copy-start(f32[256,512]{1,0:T(8,128)S(1)} %all_gather.9.refs_2_.refs_0_) | copy-start | bytes 1572868
  21.6 25.1 %collective-permute-start = (f32[256,512]{1,0:T(8,128)S(1)}, f32[256,512]{1,0:T(8,128)S(1)}, u32[]{:S(2)}, u32[]{:S(2)}) collective-permute-start(f32[256,512]{1,0:T(8,128)S(1)} %all_gather.9.refs_2_.refs_0_), channel_id=1, source_target_pairs={{0,4},{1,5},{2,6},{3,7},{4,8},{5,9},{6,10},{7,11},{8,12},{9,13},{1... | collective-permute-start | bytes 1572872 | tf_op jit(solution)/shard_map/ppermute | solution.py:49
  37.4 41.2 %copy-start = (f32[8,64,512]{2,1,0:T(8,128)}, f32[8,64,512]{2,1,0:T(8,128)S(1)}, u32[]{:S(2)}) copy-start(f32[8,64,512]{2,1,0:T(8,128)S(1)} %all-to-all-done) | copy-start | bytes 3145732
  37.4 28.6 %collective-permute-start.6 = (f32[512,512]{1,0:T(8,128)S(1)}, f32[512,512]{1,0:T(8,128)S(1)}, u32[]{:S(2)}, u32[]{:S(2)}) collective-permute-start(f32[512,512]{1,0:T(8,128)S(1)} %bitcast.23), channel_id=1, source_target_pairs={{0,1},{1,2},{2,3},{3,0},{4,5},{5,6},{6,7},{7,4},{8,9},{9,10},{10,1... | collective-permute-start | bytes 3145736 | tf_op jit(solution)/shard_map/ppermute | solution.py:44
  42.3 14.5 %collective-permute-start.3 = (f32[256,512]{1,0:T(8,128)S(1)}, f32[256,512]{1,0:T(8,128)S(1)}, u32[]{:S(2)}, u32[]{:S(2)}) collective-permute-start(f32[256,512]{1,0:T(8,128)S(1)} %all_gather.9.refs_2_.refs_0_), channel_id=1, source_target_pairs={{0,28},{1,29},{2,30},{3,31},{4,0},{5,1},{6,2},{7,3},{8,4},{9,5},{1... | collective-permute-start | bytes 1572872 | tf_op jit(solution)/shard_map/ppermute | solution.py:49
  46.7 35.7 %copy-start.3 = (f32[256,512]{1,0:T(8,128)}, f32[256,512]{1,0:T(8,128)S(1)}, u32[]{:S(2)}) copy-start(f32[256,512]{1,0:T(8,128)S(1)} %collective-permute-done.refs_6_.refs_2_) | copy-start | bytes 1572868
  46.7 15.1 %collective-permute-start.1 = (f32[256,512]{1,0:T(8,128)S(1)}, f32[256,512]{1,0:T(8,128)S(1)}, u32[]{:S(2)}, u32[]{:S(2)}) collective-permute-start(f32[256,512]{1,0:T(8,128)S(1)} %collective-permute-done.refs_6_.refs_2_), channel_id=1, source_target_pairs={{0,4},{1,5},{2,6},{3,7},{4,8},{5,9},{6,10},{7,11},{8,12},{9,13},{1... | collective-permute-start | bytes 1572872 | tf_op jit(solution)/shard_map/ppermute | solution.py:49
  48.6 33.8 %collective-permute-start.9 = (f32[512,512]{1,0:T(8,128)S(1)}, f32[512,512]{1,0:T(8,128)}, u32[]{:S(2)}, u32[]{:S(2)}) collective-permute-start(f32[512,512]{1,0:T(8,128)S(1)} %bitcast.24), channel_id=1, source_target_pairs={{0,3},{1,0},{2,1},{3,2},{4,7},{5,4},{6,5},{7,6},{8,11},{9,8},{10,9... | collective-permute-start | bytes 3145736 | tf_op jit(solution)/shard_map/ppermute | solution.py:44
  56.7 9.2 %copy-start.4 = (f32[256,512]{1,0:T(8,128)}, f32[256,512]{1,0:T(8,128)S(1)}, u32[]{:S(2)}) copy-start(f32[256,512]{1,0:T(8,128)S(1)} %collective-permute-done.3.refs_7_.refs_3_) | copy-start | bytes 1572868
  56.7 13.6 %collective-permute-start.4 = (f32[256,512]{1,0:T(8,128)S(1)}, f32[256,512]{1,0:T(8,128)}, u32[]{:S(2)}, u32[]{:S(2)}) collective-permute-start(f32[256,512]{1,0:T(8,128)S(1)} %collective-permute-done.3.refs_7_.refs_3_), channel_id=1, source_target_pairs={{0,28},{1,29},{2,30},{3,31},{4,0},{5,1},{6,2},{7,3},{8,4},{9,5},{1... | collective-permute-start | bytes 1572872 | tf_op jit(solution)/shard_map/ppermute | solution.py:49
  61.8 8.6 %copy-start.5 = (f32[256,512]{1,0:T(8,128)}, f32[256,512]{1,0:T(8,128)S(1)}, u32[]{:S(2)}) copy-start(f32[256,512]{1,0:T(8,128)S(1)} %collective-permute-done.1.refs_8_.refs_4_) | copy-start | bytes 1572868
  61.8 14.2 %collective-permute-start.2 = (f32[256,512]{1,0:T(8,128)S(1)}, f32[256,512]{1,0:T(8,128)}, u32[]{:S(2)}, u32[]{:S(2)}) collective-permute-start(f32[256,512]{1,0:T(8,128)S(1)} %collective-permute-done.1.refs_8_.refs_4_), channel_id=1, source_target_pairs={{0,4},{1,5},{2,6},{3,7},{4,8},{5,9},{6,10},{7,11},{8,12},{9,13},{1... | collective-permute-start | bytes 1572872 | tf_op jit(solution)/shard_map/ppermute | solution.py:49
  65.9 16.5 %copy-start.2 = (f32[512,512]{1,0:T(8,128)}, f32[512,512]{1,0:T(8,128)S(1)}, u32[]{:S(2)}) copy-start(f32[512,512]{1,0:T(8,128)S(1)} %collective-permute-done.6.refs_10_.refs_6_) | copy-start | bytes 3145732
  65.9 26.2 %collective-permute-start.7 = (f32[512,512]{1,0:T(8,128)S(1)}, f32[512,512]{1,0:T(8,128)}, u32[]{:S(2)}, u32[]{:S(2)}) collective-permute-start(f32[512,512]{1,0:T(8,128)S(1)} %collective-permute-done.6.refs_10_.refs_6_), channel_id=1, source_target_pairs={{0,1},{1,2},{2,3},{3,0},{4,5},{5,6},{6,7},{7,4},{8,9},{9,10},{10,1... | collective-permute-start | bytes 3145736 | tf_op jit(solution)/shard_map/ppermute | solution.py:44
  70.4 18.2 %collective-permute-start.5 = (f32[256,512]{1,0:T(8,128)}, f32[256,512]{1,0:T(8,128)}, u32[]{:S(2)}, u32[]{:S(2)}) collective-permute-start(f32[256,512]{1,0:T(8,128)} %collective-permute-done.4.refs_9_.refs_5_), channel_id=1, source_target_pairs={{0,28},{1,29},{2,30},{3,31},{4,0},{5,1},{6,2},{7,3},{8,4},{9,5},{1... | collective-permute-start | bytes 1572872 | tf_op jit(solution)/shard_map/ppermute | solution.py:49
  76.0 13.5 %collective-permute-start.8 = (f32[256,512]{1,0:T(8,128)}, f32[256,512]{1,0:T(8,128)}, u32[]{:S(2)}, u32[]{:S(2)}) collective-permute-start(f32[256,512]{1,0:T(8,128)} %collective-permute-done.2.refs_4_.refs_8_), channel_id=1, source_target_pairs={{0,4},{1,5},{2,6},{3,7},{4,8},{5,9},{6,10},{7,11},{8,12},{9,13},{1... | collective-permute-start | bytes 1572872 | tf_op jit(solution)/shard_map/ppermute | solution.py:49

commit v4 on v3

v4 whole, which is shorter than its diff:
```python
import functools

import jax
import jax.numpy as jnp
from jax import lax
from jax.experimental import pallas as pl
from jax.experimental.pallas import tpu as pltpu
from jax.sharding import PartitionSpec as P

BLOCK = 64
NX = 4
NY = 8
AHEAD = 4
ROWS_A = 64
VMEM_INNER = 16 * 1024 * 1024
VMEM_UPDATE = 24 * 1024 * 1024


def split(value):
    high = value.astype(jnp.bfloat16)
    low = (value - high.astype(jnp.float32)).astype(jnp.bfloat16)
    return high, low


def dot(left, right):
    return jnp.dot(left, right, preferred_element_type=jnp.float32)


def shape_own(drawn, row_index, col_index, row_count):
    panels, rows, width = drawn.shape
    local_rows = col_index * rows + jnp.arange(rows, dtype=jnp.int32)
    matrix_rows = local_rows // BLOCK * BLOCK * row_count + row_index * BLOCK + local_rows % BLOCK
    matrix_rows = matrix_rows[None, :, None]
    diagonal_at = (
        jnp.arange(panels, dtype=jnp.int32)[:, None, None] * width
        + jnp.arange(width, dtype=jnp.int32)[None, None, :]
    )
    return jnp.where(
        matrix_rows < diagonal_at,
        jnp.float32(0.0),
        jnp.where(matrix_rows == diagonal_at, jnp.float32(1.0), drawn),
    )


def move_x(value, shift):
    pairs = [(y * NX + x, y * NX + (x + shift) % NX) for y in range(NY) for x in range(NX)]
    return lax.ppermute(value, "col", pairs)


def move_y(value, shift):
    pairs = [(y * NX + x, (y + shift) % NY * NX + x) for y in range(NY) for x in range(NX)]
    return lax.ppermute(value, "col", pairs)


GROUPS_X = [[y * NX + x for x in range(NX)] for y in range(NY)]
GROUPS_Y = [[y * NX + x for y in range(NY)] for x in range(NX)]


def spread(value, groups):
    count = len(groups[0])
    copies = jnp.broadcast_to(value[None], (count,) + value.shape)
    return lax.all_to_all(copies, "col", 0, 0, axis_index_groups=groups)


SHIFTS_B = [0, -1, 1, NX // 2]
SHIFTS_A = [0, -1, 1, -2, 2, -3, 3, NY // 2]


def eig_a(y):
    return pl.ds(y, 1), pl.ds(0, NX), pl.ds(0, ROWS_A)


def eig_b(x, rows):
    return pl.ds(0, NY), pl.ds(x, 1), pl.ds(ROWS_A, rows - ROWS_A)


def pieces_of(at_ref, shifts, rows):
    places = [eig_b(at_ref[SHIFTS_B.index(shift)], rows) for shift in shifts[0]]
    return places + [eig_a(at_ref[NX + SHIFTS_A.index(shift)]) for shift in shifts[1]]


def load(source, target, sem):
    copy = pltpu.make_async_copy(source, target, sem)
    copy.start()
    return copy


def add_products(inner_ref, gram_ref, eig, panel):
    cols = eig.shape[1]
    width = panel.shape[1] // 2
    high, low = split(eig.T)
    parts = jnp.concatenate([high, low], axis=0)
    panel_high, panel_low = split(panel)
    both = dot(parts, panel_high)
    inner_ref[...] += both[:cols] + (both[cols:] + dot(high, panel_low))
    high = panel_high[:, width:].T
    low = panel_low[:, width:].T
    gram_ref[...] += dot(high, panel_high[:, :width]) + (
        dot(low, panel_high[:, :width]) + dot(high, panel_low[:, :width])
    )


def whole(value):
    return pl.BlockSpec(value.shape, lambda i, at_ref: (0,) * len(value.shape))


def inner_kernel(shifts, first, last, at_ref, eig_ref, *refs):
    count = len(shifts[0]) + len(shifts[1])
    panels, refs = refs[:count], refs[count:]
    if first:
        starts = None
    else:
        starts, refs = refs[:2], refs[2:]
    outs, (inner_ref, gram_ref) = refs[:-2], refs[-2:]
    inner_ref[...] = jnp.zeros_like(inner_ref) if first else starts[0][...]
    gram_ref[...] = jnp.zeros_like(gram_ref) if first else starts[1][...]
    for panel_ref, where in zip(panels, pieces_of(at_ref, shifts, eig_ref.shape[2])):
        eig = eig_ref[where]
        add_products(inner_ref, gram_ref, eig.reshape(-1, eig.shape[-1]), panel_ref[...])
    if not last:
        outs[0][...] = inner_ref[...]
        outs[1][...] = gram_ref[...]
        return
    (out_ref,) = outs
    shares, share, width = out_ref.shape
    half = gram_ref.shape[0] // 2
    out_ref[:, : share // 2, :] = inner_ref[...].reshape(shares, share // 2, width)
    gram = jnp.concatenate([gram_ref[:half, :], gram_ref[half:, :]], axis=1)
    out_ref[:, share // 2 :, :] = gram.reshape(shares, share // 2, width)


def inner_products(at, eigs, shifts, panels, starts, shares):
    cols = eigs.shape[3]
    width = panels[0].shape[1]
    total = sum(panel.shape[0] for panel in panels)
    state = [jax.ShapeDtypeStruct(shape, jnp.float32) for shape in [(cols, width), (width // 2, width // 2)]]
    outs = [jax.ShapeDtypeStruct((shares, 2 * cols // shares, width), jnp.float32)] if shares else state
    args = [eigs, *panels] + ([] if starts is None else list(starts))
    return pl.pallas_call(
        functools.partial(inner_kernel, shifts, starts is None, bool(shares)),
        grid_spec=pltpu.PrefetchScalarGridSpec(
            num_scalar_prefetch=1,
            grid=(1,),
            in_specs=[whole(arg) for arg in args],
            out_specs=[whole(out) for out in outs],
            scratch_shapes=[pltpu.VMEM(shape.shape, jnp.float32) for shape in state],
        ),
        out_shape=outs,
        compiler_params=pltpu.CompilerParams(vmem_limit_bytes=VMEM_INNER),
        cost_estimate=pl.CostEstimate(
            flops=12 * total * cols * width, bytes_accessed=4 * total * (width + cols), transcendentals=0
        ),
    )(at, *args)


def times(left, right):
    return lax.dot_general(
        left,
        right,
        (((1,), (1,)), ((), ())),
        precision=lax.Precision.HIGHEST,
        preferred_element_type=jnp.float32,
    )


def triangle(tau):
    row = lax.broadcasted_iota(jnp.int32, tau.shape, 0)
    col = lax.broadcasted_iota(jnp.int32, tau.shape, 1)
    return jnp.where(row < col, tau, jnp.where(row == col, jnp.float32(1.0), jnp.float32(0.0)))


def update_kernel(at_ref, sums_ref, tau_hbm, eig_hbm, *refs):
    panels, out_ref = refs[: NX + NY], refs[NX + NY]
    parts_ref, tau_ref, eig_ref, buf_ref, own_sems, sems, out_sems = refs[NX + NY + 1 :]
    rows, cols = eig_ref.shape[2:]
    width = tau_ref.shape[1]
    tau_load = load(tau_hbm, tau_ref, own_sems.at[0])
    eig_load = load(eig_hbm, eig_ref, own_sems.at[1])
    spans = [0]
    for panel_ref in panels:
        spans.append(spans[-1] + panel_ref.shape[0])

    def start(n):
        return load(panels[n], buf_ref.at[pl.ds(spans[n], panels[n].shape[0])], sems.at[n])

    copies = [start(n) for n in range(AHEAD)]
    tau_load.wait()
    own_cols = sums_ref.shape[1] // 2
    inner = sums_ref[:, :own_cols, :].reshape(cols, 2 * width)
    gram = sums_ref[:, own_cols:, :].reshape(cols, 2 * width)
    gram = jnp.concatenate([gram[:, :width], gram[:, width:]], axis=0)
    s_two = times(inner[:, :width], triangle(tau_ref[1]))
    s_one = times(inner[:, width:] - times(s_two, gram), triangle(tau_ref[0]))
    high, low = split(jnp.concatenate([s_two, s_one], axis=1).T)
    parts_ref[:, :cols] = high
    parts_ref[:, cols:] = low

    eig_load.wait()
    stores = []
    for n, where in enumerate(pieces_of(at_ref, (SHIFTS_B, SHIFTS_A), rows)):
        copies[n].wait()
        if n + AHEAD < len(panels):
            copies.append(start(n + AHEAD))
        high, low = split(buf_ref[spans[n] : spans[n + 1], :])
        both = dot(high, parts_ref[...])
        change = both[:, :cols] + (both[:, cols:] + dot(low, parts_ref[:, :cols]))
        old = eig_ref[where]
        eig_ref[where] = old - change.reshape(old.shape)
        if n >= NX:
            stores.append(load(eig_ref.at[where[0]], out_ref.at[where[0]], out_sems.at[n - NX]))
    for copy in stores:
        copy.wait()


def in_hbm(value):
    return pltpu.with_memory_space_constraint(value, pltpu.HBM)


def update(at, eigs, sums, tau, panels):
    cols = eigs.shape[3]
    width = panels[0].shape[1]
    total = sum(panel.shape[0] for panel in panels)
    anywhere = pl.BlockSpec(memory_space=pl.ANY)
    return pl.pallas_call(
        update_kernel,
        grid_spec=pltpu.PrefetchScalarGridSpec(
            num_scalar_prefetch=1,
            grid=(1,),
            in_specs=[whole(sums)] + [anywhere] * (2 + len(panels)),
            out_specs=anywhere,
            scratch_shapes=[
                pltpu.VMEM((width, 2 * cols), jnp.bfloat16),
                pltpu.VMEM(tau.shape, jnp.float32),
                pltpu.VMEM(eigs.shape, jnp.float32),
                pltpu.VMEM((total, width), jnp.float32),
                pltpu.SemaphoreType.DMA((2,)),
                pltpu.SemaphoreType.DMA((NX + NY,)),
                pltpu.SemaphoreType.DMA((NY,)),
            ],
        ),
        out_shape=jax.ShapeDtypeStruct(eigs.shape, jnp.float32),
        compiler_params=pltpu.CompilerParams(vmem_limit_bytes=VMEM_UPDATE),
        cost_estimate=pl.CostEstimate(
            flops=6 * total * cols * width, bytes_accessed=4 * total * (width + 2 * cols), transcendentals=0
        ),
    )(at, sums, in_hbm(tau), in_hbm(eigs), *[in_hbm(panel) for panel in panels])


def shards(eigvecs, reflectors, tau_blocks):
    row_index = lax.axis_index("row")
    col_index = lax.axis_index("col")
    row_count = lax.axis_size("row")
    width = 2 * tau_blocks.shape[1]
    y_at, x_at = (col_index // NX).astype(jnp.int32), (col_index % NX).astype(jnp.int32)
    at = jnp.concatenate(
        [(x_at + NX + jnp.array(SHIFTS_B, jnp.int32)) % NX, (y_at + NY + jnp.array(SHIFTS_A, jnp.int32)) % NY]
    )
    eigs = eigvecs.reshape(NY, NX, reflectors.shape[1], eigvecs.shape[1])

    own = shape_own(reflectors, row_index, col_index, row_count)
    own = jnp.concatenate([own[1], own[0]], axis=1)

    own_a = lax.all_gather(own[:ROWS_A], "col", axis=0, tiled=True, axis_index_groups=GROUPS_X)
    own_b = spread(own[ROWS_A:], GROUPS_Y).reshape(-1, width)
    own_b, _ = lax.optimization_barrier((own_b, own_a))
    up, down = [own_a], [own_a]
    for _ in range(NY // 2 - 1):
        up.append(move_y(up[-1], 1))
        down.append(move_y(down[-1], -1))
    far_a = move_y(up[-1], 1)
    left, right = move_x(own_b, 1), move_x(own_b, -1)
    far_b = move_x(left, 1)

    state = inner_products(at, eigs, ([0], [0, -1, 1]), [own_b, own_a, up[1], down[1]], None, 0)
    state = inner_products(at, eigs, ([-1, 1], [-2, 2]), [left, right, up[2], down[2]], state, 0)
    (shares,) = inner_products(
        at, eigs, ([NX // 2], [-3, 3, NY // 2]), [far_b, up[3], down[3], far_a], state, row_count
    )
    share = jnp.sum(lax.all_to_all(shares, "row", 0, 0), axis=0)
    sums = lax.all_gather(share, "row")

    panels = [own_b, left, right, far_b, own_a, up[1], down[1], up[2], down[2], up[3], down[3], far_a]
    return update(at, eigs, sums, tau_blocks, panels).reshape(eigvecs.shape)


def solution(mesh):
    in_specs = (P("row", "col"), P(None, ("row", "col"), None), P())
    out_specs = P("row", "col")
    return jax.shard_map(shards, mesh=mesh, in_specs=in_specs, out_specs=out_specs, check_vma=False)
```

time: 154 us -> 152 us (0.987)
  Pallas kernels: 23.6 us -> 19.4 us
  waiting for transfers between devices: 29.1 us -> 31.8 us
    ppermute x7, waiting for transfers between devices: 11.8 us -> 16 us  [move_y(): return lax.ppermute(value, 'col', pairs)]
    pallas_call x4, Pallas kernels: 23.6 us -> 19.4 us  [the longest x3 10.2 us: inner_products(): pl.pallas_call(functools.partial(inner_kernel, shifts, starts is None, bo...]
  transfers between devices with their start and end apart: 11 -> 11, of which waited for: 9 -> 9; matrix products, arithmetic and copies ran while one was open for 0% -> 0% of each run, Pallas kernels for 6% -> 5%
where the time goes in v4:
time: 152 us; the launch traced here: 151 us
  blocking collectives  58.4 us (38%)
  starting transfers between devices  38.8 us (26%)
  waiting for transfers between devices  31.8 us (21%)
  Pallas kernels  19.4 us (13%)
    all_to_all x1, blocking collectives, shards(): share = jnp.sum(lax.all_to_all(shares, 'row', 0, 0), axis=0)  30.4 us
    ppermute x7, starting transfers between devices, move_y(): return lax.ppermute(value, 'col', pairs)  19.7 us
    ppermute x7, waiting for transfers between devices, move_y(): return lax.ppermute(value, 'col', pairs)  16 us
    all_gather x1, blocking collectives, shards(): sums = lax.all_gather(share, 'row')  15.9 us
    all_gather x1, blocking collectives, shards(): lax.all_gather(own[:ROWS_A], 'col', axis=0, tiled=True, axis_index_groups...  12.2 us
    all_to_all x1, waiting for transfers between devices, spread(): return lax.all_to_all(copies, 'col', 0, 0, axis_index_groups=groups)  11.6 us
    ppermute x3, starting transfers between devices, move_x(): return lax.ppermute(value, 'col', pairs)  11.5 us
    pallas_call x3, Pallas kernels, inner_products(): pl.pallas_call(functools.partial(inner_kernel, shifts, starts is None, bo...  10.2 us
  transfers between devices with their start and end apart: 11, of which 9 were waited for; matrix products, arithmetic and copies ran while one was open for 0% of the time, Pallas kernels for 5%

profile of v4, /device:TPU:1, one launch (start us, length us, event | category | flops | bytes accessed | tf_op | source)
XLA Modules:
  0.0 151.2 jit_solution(11481281696284713576)
XLA Ops:
  0.0 0.1 iota_add_fusion
  0.1 1.1 select_select_fusion
  1.2 0.0 copy-start.5
  1.2 1.1 broadcast_in_dim.18
  2.3 7.7 %all-to-all-start = ((f32[8,64,512]{2,1,0:T(8,128)}), f32[8,64,512]{2,1,0:T(8,128)S(1)}, u32[]{:S(2)}, u32[]{:S(2)}) async-start(f32[8,64,512]{2,1,0:T(8,128)} %broadcast_in_dim.18), calls=%async_computation | async-start | bytes 2097152 | tf_op jit(solution)/shard_map/all_to_all | solution.py:62
  10.0 12.2 %all_gather.9.refs_1_.refs_4_ = f32[256,512]{1,0:T(8,128)} all-gather(f32[64,512]{1,0:T(8,128)S(1)} %get-tuple-element.15), channel_id=1, replica_groups={{0,1,2,3},{4,5,6,7},{8,9,10,11},{12,13,14,15},{16,17,18,19},{20,21,22,2..., dimensions={0}, use_global_device_ids=true | all-gather | bytes 655360 | tf_op jit(solution)/shard_map/all_gather | solution.py:263
  22.2 3.6 %collective-permute-start.2 = (f32[256,512]{1,0:T(8,128)}, f32[256,512]{1,0:T(8,128)}, u32[]{:S(2)}, u32[]{:S(2)}) collective-permute-start(f32[256,512]{1,0:T(8,128)} %all_gather.9.refs_1_.refs_4_), channel_id=1, source_target_pairs={{0,4},{1,5},{2,6},{3,7},{4,8},{5,9},{6,10},{7,11},{8,12},{9,13},{1... | collective-permute-start | bytes 1572872 | tf_op jit(solution)/shard_map/ppermute | solution.py:52
  25.8 11.6 %all-to-all-done = f32[8,64,512]{2,1,0:T(8,128)S(1)} async-done(((f32[8,64,512]{2,1,0:T(8,128)}), f32[8,64,512]{2,1,0:T(8,128)S(1)}, u32[]{:S(2)}, u32[]{:S(2)}) %all-to-all-start) | async-done | bytes 1048608 | tf_op jit(solution)/shard_map/all_to_all | solution.py:62
  37.4 4.9 %collective-permute-start = (f32[512,512]{1,0:T(8,128)S(1)}, f32[512,512]{1,0:T(8,128)}, u32[]{:S(2)}, u32[]{:S(2)}) collective-permute-start(f32[512,512]{1,0:T(8,128)S(1)} %bitcast.12), channel_id=1, source_target_pairs={{0,1},{1,2},{2,3},{3,0},{4,5},{5,6},{6,7},{7,4},{8,9},{9,10},{10,1... | collective-permute-start | bytes 3145736 | tf_op jit(solution)/shard_map/ppermute | solution.py:47
  42.3 1.9 %collective-permute-start.5 = (f32[256,512]{1,0:T(8,128)}, f32[256,512]{1,0:T(8,128)}, u32[]{:S(2)}, u32[]{:S(2)}) collective-permute-start(f32[256,512]{1,0:T(8,128)} %all_gather.9.refs_1_.refs_4_), channel_id=1, source_target_pairs={{0,28},{1,29},{2,30},{3,31},{4,0},{5,1},{6,2},{7,3},{8,4},{9,5},{1... | collective-permute-start | bytes 1572872 | tf_op jit(solution)/shard_map/ppermute | solution.py:52
  44.2 2.6 %collective-permute-done.2.refs_2_.refs_5_ = f32[256,512]{1,0:T(8,128)} collective-permute-done((f32[256,512]{1,0:T(8,128)}, f32[256,512]{1,0:T(8,128)}, u32[]{:S(2)}, u32[]{:S(2)}) %collective-permute-start.2) | collective-permute-done | bytes 524320 | tf_op jit(solution)/shard_map/ppermute | solution.py:52
  46.9 1.9 %collective-permute-start.3 = (f32[256,512]{1,0:T(8,128)}, f32[256,512]{1,0:T(8,128)}, u32[]{:S(2)}, u32[]{:S(2)}) collective-permute-start(f32[256,512]{1,0:T(8,128)} %collective-permute-done.2.refs_2_.refs_5_), channel_id=1, source_target_pairs={{0,4},{1,5},{2,6},{3,7},{4,8},{5,9},{6,10},{7,11},{8,12},{9,13},{1... | collective-permute-start | bytes 1572872 | tf_op jit(solution)/shard_map/ppermute | solution.py:52
  48.8 4.4 %collective-permute-start.9 = (f32[512,512]{1,0:T(8,128)S(1)}, f32[512,512]{1,0:T(8,128)}, u32[]{:S(2)}, u32[]{:S(2)}) collective-permute-start(f32[512,512]{1,0:T(8,128)S(1)} %bitcast.13), channel_id=1, source_target_pairs={{0,3},{1,0},{2,1},{3,2},{4,7},{5,4},{6,5},{7,6},{8,11},{9,8},{10,9... | collective-permute-start | bytes 3145736 | tf_op jit(solution)/shard_map/ppermute | solution.py:47
  53.2 3.8 %collective-permute-done.5.refs_3_.refs_6_ = f32[256,512]{1,0:T(8,128)} collective-permute-done((f32[256,512]{1,0:T(8,128)}, f32[256,512]{1,0:T(8,128)}, u32[]{:S(2)}, u32[]{:S(2)}) %collective-permute-start.5) | collective-permute-done | bytes 524320 | tf_op jit(solution)/shard_map/ppermute | solution.py:52
  57.0 3.4 %collective-permute-start.6 = (f32[256,512]{1,0:T(8,128)}, f32[256,512]{1,0:T(8,128)}, u32[]{:S(2)}, u32[]{:S(2)}) collective-permute-start(f32[256,512]{1,0:T(8,128)} %collective-permute-done.5.refs_3_.refs_6_), channel_id=1, source_target_pairs={{0,28},{1,29},{2,30},{3,31},{4,0},{5,1},{6,2},{7,3},{8,4},{9,5},{1... | collective-permute-start | bytes 1572872 | tf_op jit(solution)/shard_map/ppermute | solution.py:52
  60.4 1.8 %collective-permute-done.3.refs_2_.refs_7_ = f32[256,512]{1,0:T(8,128)} collective-permute-done((f32[256,512]{1,0:T(8,128)}, f32[256,512]{1,0:T(8,128)}, u32[]{:S(2)}, u32[]{:S(2)}) %collective-permute-start.3) | collective-permute-done | bytes 524320 | tf_op jit(solution)/shard_map/ppermute | solution.py:52
  62.2 1.9 %collective-permute-start.4 = (f32[256,512]{1,0:T(8,128)}, f32[256,512]{1,0:T(8,128)}, u32[]{:S(2)}, u32[]{:S(2)}) collective-permute-start(f32[256,512]{1,0:T(8,128)} %collective-permute-done.3.refs_2_.refs_7_), channel_id=1, source_target_pairs={{0,4},{1,5},{2,6},{3,7},{4,8},{5,9},{6,10},{7,11},{8,12},{9,13},{1... | collective-permute-start | bytes 1572872 | tf_op jit(solution)/shard_map/ppermute | solution.py:52
  64.2 1.9 %collective-permute-done.refs_0_.refs_1_ = f32[512,512]{1,0:T(8,128)} collective-permute-done((f32[512,512]{1,0:T(8,128)S(1)}, f32[512,512]{1,0:T(8,128)}, u32[]{:S(2)}, u32[]{:S(2)}) %collective-permute-start) | collective-permute-done | bytes 1048608 | tf_op jit(solution)/shard_map/ppermute | solution.py:47
  66.1 2.2 %collective-permute-start.1 = (f32[512,512]{1,0:T(8,128)}, f32[512,512]{1,0:T(8,128)}, u32[]{:S(2)}, u32[]{:S(2)}) collective-permute-start(f32[512,512]{1,0:T(8,128)} %collective-permute-done.refs_0_.refs_1_), channel_id=1, source_target_pairs={{0,1},{1,2},{2,3},{3,0},{4,5},{5,6},{6,7},{7,4},{8,9},{9,10},{10,1... | collective-permute-start | bytes 3145736 | tf_op jit(solution)/shard_map/ppermute | solution.py:47
  68.4 2.4 %collective-permute-done.6.refs_3_.refs_8_ = f32[256,512]{1,0:T(8,128)} collective-permute-done((f32[256,512]{1,0:T(8,128)}, f32[256,512]{1,0:T(8,128)}, u32[]{:S(2)}, u32[]{:S(2)}) %collective-permute-start.6) | collective-permute-done | bytes 524320 | tf_op jit(solution)/shard_map/ppermute | solution.py:52
  70.7 5.0 %collective-permute-start.7 = (f32[256,512]{1,0:T(8,128)}, f32[256,512]{1,0:T(8,128)S(1)}, u32[]{:S(2)}, u32[]{:S(2)}) collective-permute-start(f32[256,512]{1,0:T(8,128)} %collective-permute-done.6.refs_3_.refs_8_), channel_id=1, source_target_pairs={{0,28},{1,29},{2,30},{3,31},{4,0},{5,1},{6,2},{7,3},{8,4},{9,5},{1... | collective-permute-start | bytes 1572872 | tf_op jit(solution)/shard_map/ppermute | solution.py:52
  75.7 1.0 collective-permute-done.4.refs_1_.refs_9_
  76.7 1.9 %collective-permute-start.8 = (f32[256,512]{1,0:T(8,128)}, f32[256,512]{1,0:T(8,128)S(1)}, u32[]{:S(2)}, u32[]{:S(2)}) collective-permute-start(f32[256,512]{1,0:T(8,128)} %collective-permute-done.4.refs_1_.refs_9_), channel_id=1, source_target_pairs={{0,4},{1,5},{2,6},{3,7},{4,8},{5,9},{6,10},{7,11},{8,12},{9,13},{1... | collective-permute-start | bytes 1572872 | tf_op jit(solution)/shard_map/ppermute | solution.py:52
  78.6 0.1 pad_add_fusion.at_ref
  78.7 3.1 %shard_map.55 = (f32[128,512]{1,0:T(8,128)S(1)}, f32[256,256]{1,0:T(8,128)S(1)}) custom-call(s32[12]{0:T(128)S(1)} %pad_add_fusion.at_ref, f32[8,4,128,128]{3,2,1,0:T(8,128)S(1)} %bitcast.9, f32[512,512]{1,0:T(8,128)S(1)} %bitcast.14, f32[256,512]{1,0:T(8,128)} %all_gather.9.refs_1_.refs_4_, f32[256,512]{1,0:T(8,128)} %collective-permute-done.2.refs_2_.refs_5_, ...), custom_call_target="tpu_custom_call" | custom-call | flops 1006632960 | bytes 3276800 | tf_op jit(solution)/shard_map/pallas_call | solution.py:139
  81.9 3.8 %shard_map.56 = (f32[128,512]{1,0:T(8,128)S(1)}, f32[256,256]{1,0:T(8,128)S(1)}) custom-call(s32[12]{0:T(128)S(1)} %pad_add_fusion.at_ref, f32[8,4,128,128]{3,2,1,0:T(8,128)S(1)} %bitcast.10, f32[512,512]{1,0:T(8,128)} %collective-permute-done.refs_0_.refs_1_, f32[512,512]{1,0:T(8,128)} %collective-permute-done.9.refs_1_.refs_2_, ...), custom_call_target="tpu_custom_call" | custom-call | flops 1207959552 | bytes 3932160 | tf_op jit(solution)/shard_map/pallas_call | solution.py:139
  85.7 4.5 %collective-permute-done.8.refs_3_.refs_11_ = f32[256,512]{1,0:T(8,128)S(1)} collective-permute-done((f32[256,512]{1,0:T(8,128)}, f32[256,512]{1,0:T(8,128)S(1)}, u32[]{:S(2)}, u32[]{:S(2)}) %collective-permute-start.8) | collective-permute-done | bytes 524320 | tf_op jit(solution)/shard_map/ppermute | solution.py:52
  90.2 2.2 %collective-permute-done.1.refs_0_.refs_3_ = f32[512,512]{1,0:T(8,128)} collective-permute-done((f32[512,512]{1,0:T(8,128)}, f32[512,512]{1,0:T(8,128)}, u32[]{:S(2)}, u32[]{:S(2)}) %collective-permute-start.1) | collective-permute-done | bytes 1048608 | tf_op jit(solution)/shard_map/ppermute | solution.py:47
  92.4 3.2 %shard_map.57 = f32[16,16,512]{2,1,0:T(8,128)S(1)} custom-call(s32[12]{0:T(128)S(1)} %pad_add_fusion.at_ref, f32[8,4,128,128]{3,2,1,0:T(8,128)S(1)} %bitcast.11, f32[512,512]{1,0:T(8,128)} %collective-permute-done.1.refs_0_.refs_3_, f32[256,512]{1,0:T(8,128)} %collective-permute-done.4.refs_1_.refs_9_, ...), custom_call_target="tpu_custom_call" | custom-call | flops 1006632960 | bytes 3276800 | tf_op jit(solution)/shard_map/pallas_call | solution.py:139
  95.6 30.4 %all_to_all.10 = f32[16,16,512]{2,1,0:T(8,128)S(1)} all-to-all(f32[16,16,512]{2,1,0:T(8,128)S(1)} %shard_map.57), channel_id=1, replica_groups=mesh['row'=16,'col'=32] {'row'}, dimensions={0} | all-to-all | bytes 1048576 | tf_op jit(solution)/shard_map/all_to_all | solution.py:279
  126.1 15.9 %all-gather = f32[256,512]{1,0:T(8,128)S(1)} all-gather(f32[16,512]{1,0:T(8,128)S(1)} %reduce_sum.9), channel_id=2, replica_groups=mesh['row'=16,'col'=32] {'row'}, dimensions={0}, use_global_device_ids=true | all-gather | bytes 557056 | tf_op jit(solution)/shard_map/all_gather | solution.py:280
  142.0 9.2 %shard_map.58 = f32[8,4,128,128]{3,2,1,0:T(8,128)} custom-call(s32[12]{0:T(128)S(1)} %pad_add_fusion.at_ref, f32[16,16,512]{2,1,0:T(8,128)S(1)} %bitcast.16, f32[2,256,256]{2,1,0:T(8,128)} %tau_hbm.1, f32[8,4,128,128]{3,2,1,0:T(8,128)} %bitcast.8, f32[512,512]{1,0:T(8,128)} %bitcast.15, f32[512,512]{1,0:T(8,128)} %collective-permute-done.refs_0_.refs_1_, ...), custom_call_target="tpu_custom_call" | custom-call | flops 1610612736 | bytes 12582912 | tf_op jit(solution)/shard_map/pallas_call | solution.py:224
  (20 shorter events, 0.1 us)
Async XLA Ops:
  1.2 67.1 %copy-start.5 = (s32[8]{0:T(128)S(1)}, s32[8]{0:T(128)}, u32[]{:S(2)}) copy-start(s32[8]{0:T(128)} %constant.99.clone) | copy-start | bytes 100
  1.2 77.4 %copy-start.4 = (s32[4]{0:T(128)S(1)}, s32[4]{0:T(128)}, u32[]{:S(2)}) copy-start(s32[4]{0:T(128)} %constant.98.clone) | copy-start | bytes 52
  1.2 77.5 %copy-start = (f32[4096,128]{1,0:T(8,128)S(1)}, f32[4096,128]{1,0:T(8,128)}, u32[]{:S(2)}) copy-start(f32[4096,128]{1,0:T(8,128)} %param.5) | copy-start | bytes 6291460
  2.3 35.1 %all-to-all-start = ((f32[8,64,512]{2,1,0:T(8,128)}), f32[8,64,512]{2,1,0:T(8,128)S(1)}, u32[]{:S(2)}, u32[]{:S(2)}) async-start(f32[8,64,512]{2,1,0:T(8,128)} %broadcast_in_dim.18), calls=%async_computation | async-start | bytes 2097152 | tf_op jit(solution)/shard_map/all_to_all | solution.py:62
  22.2 24.7 %collective-permute-start.2 = (f32[256,512]{1,0:T(8,128)}, f32[256,512]{1,0:T(8,128)}, u32[]{:S(2)}, u32[]{:S(2)}) collective-permute-start(f32[256,512]{1,0:T(8,128)} %all_gather.9.refs_1_.refs_4_), channel_id=1, source_target_pairs={{0,4},{1,5},{2,6},{3,7},{4,8},{5,9},{6,10},{7,11},{8,12},{9,13},{1... | collective-permute-start | bytes 1572872 | tf_op jit(solution)/shard_map/ppermute | solution.py:52
  37.4 44.5 %copy-start.1 = (f32[8,64,512]{2,1,0:T(8,128)}, f32[8,64,512]{2,1,0:T(8,128)S(1)}, u32[]{:S(2)}) copy-start(f32[8,64,512]{2,1,0:T(8,128)S(1)} %all-to-all-done) | copy-start | bytes 3145732
  37.4 28.7 %collective-permute-start = (f32[512,512]{1,0:T(8,128)S(1)}, f32[512,512]{1,0:T(8,128)}, u32[]{:S(2)}, u32[]{:S(2)}) collective-permute-start(f32[512,512]{1,0:T(8,128)S(1)} %bitcast.12), channel_id=1, source_target_pairs={{0,1},{1,2},{2,3},{3,0},{4,5},{5,6},{6,7},{7,4},{8,9},{9,10},{10,1... | collective-permute-start | bytes 3145736 | tf_op jit(solution)/shard_map/ppermute | solution.py:47
  42.3 14.7 %collective-permute-start.5 = (f32[256,512]{1,0:T(8,128)}, f32[256,512]{1,0:T(8,128)}, u32[]{:S(2)}, u32[]{:S(2)}) collective-permute-start(f32[256,512]{1,0:T(8,128)} %all_gather.9.refs_1_.refs_4_), channel_id=1, source_target_pairs={{0,28},{1,29},{2,30},{3,31},{4,0},{5,1},{6,2},{7,3},{8,4},{9,5},{1... | collective-permute-start | bytes 1572872 | tf_op jit(solution)/shard_map/ppermute | solution.py:52
  46.9 15.4 %collective-permute-start.3 = (f32[256,512]{1,0:T(8,128)}, f32[256,512]{1,0:T(8,128)}, u32[]{:S(2)}, u32[]{:S(2)}) collective-permute-start(f32[256,512]{1,0:T(8,128)} %collective-permute-done.2.refs_2_.refs_5_), channel_id=1, source_target_pairs={{0,4},{1,5},{2,6},{3,7},{4,8},{5,9},{6,10},{7,11},{8,12},{9,13},{1... | collective-permute-start | bytes 1572872 | tf_op jit(solution)/shard_map/ppermute | solution.py:52
  48.8 33.1 %collective-permute-start.9 = (f32[512,512]{1,0:T(8,128)S(1)}, f32[512,512]{1,0:T(8,128)}, u32[]{:S(2)}, u32[]{:S(2)}) collective-permute-start(f32[512,512]{1,0:T(8,128)S(1)} %bitcast.13), channel_id=1, source_target_pairs={{0,3},{1,0},{2,1},{3,2},{4,7},{5,4},{6,5},{7,6},{8,11},{9,8},{10,9... | collective-permute-start | bytes 3145736 | tf_op jit(solution)/shard_map/ppermute | solution.py:47
  57.0 13.7 %collective-permute-start.6 = (f32[256,512]{1,0:T(8,128)}, f32[256,512]{1,0:T(8,128)}, u32[]{:S(2)}, u32[]{:S(2)}) collective-permute-start(f32[256,512]{1,0:T(8,128)} %collective-permute-done.5.refs_3_.refs_6_), channel_id=1, source_target_pairs={{0,28},{1,29},{2,30},{3,31},{4,0},{5,1},{6,2},{7,3},{8,4},{9,5},{1... | collective-permute-start | bytes 1572872 | tf_op jit(solution)/shard_map/ppermute | solution.py:52
  62.2 14.4 %collective-permute-start.4 = (f32[256,512]{1,0:T(8,128)}, f32[256,512]{1,0:T(8,128)}, u32[]{:S(2)}, u32[]{:S(2)}) collective-permute-start(f32[256,512]{1,0:T(8,128)} %collective-permute-done.3.refs_2_.refs_7_), channel_id=1, source_target_pairs={{0,4},{1,5},{2,6},{3,7},{4,8},{5,9},{6,10},{7,11},{8,12},{9,13},{1... | collective-permute-start | bytes 1572872 | tf_op jit(solution)/shard_map/ppermute | solution.py:52
  66.1 26.4 %collective-permute-start.1 = (f32[512,512]{1,0:T(8,128)}, f32[512,512]{1,0:T(8,128)}, u32[]{:S(2)}, u32[]{:S(2)}) collective-permute-start(f32[512,512]{1,0:T(8,128)} %collective-permute-done.refs_0_.refs_1_), channel_id=1, source_target_pairs={{0,1},{1,2},{2,3},{3,0},{4,5},{5,6},{6,7},{7,4},{8,9},{9,10},{10,1... | collective-permute-start | bytes 3145736 | tf_op jit(solution)/shard_map/ppermute | solution.py:47
  70.7 15.0 %collective-permute-start.7 = (f32[256,512]{1,0:T(8,128)}, f32[256,512]{1,0:T(8,128)S(1)}, u32[]{:S(2)}, u32[]{:S(2)}) collective-permute-start(f32[256,512]{1,0:T(8,128)} %collective-permute-done.6.refs_3_.refs_8_), channel_id=1, source_target_pairs={{0,28},{1,29},{2,30},{3,31},{4,0},{5,1},{6,2},{7,3},{8,4},{9,5},{1... | collective-permute-start | bytes 1572872 | tf_op jit(solution)/shard_map/ppermute | solution.py:52
  76.7 13.5 %collective-permute-start.8 = (f32[256,512]{1,0:T(8,128)}, f32[256,512]{1,0:T(8,128)S(1)}, u32[]{:S(2)}, u32[]{:S(2)}) collective-permute-start(f32[256,512]{1,0:T(8,128)} %collective-permute-done.4.refs_1_.refs_9_), channel_id=1, source_target_pairs={{0,4},{1,5},{2,6},{3,7},{4,8},{5,9},{6,10},{7,11},{8,12},{9,13},{1... | collective-permute-start | bytes 1572872 | tf_op jit(solution)/shard_map/ppermute | solution.py:52
  85.7 9.9 %copy-start.2 = (f32[256,512]{1,0:T(8,128)}, f32[256,512]{1,0:T(8,128)S(1)}, u32[]{:S(2)}) copy-start(f32[256,512]{1,0:T(8,128)S(1)} %collective-permute-done.7.refs_2_.refs_10_) | copy-start | bytes 1572868
  90.2 5.4 %copy-start.3 = (f32[256,512]{1,0:T(8,128)}, f32[256,512]{1,0:T(8,128)S(1)}, u32[]{:S(2)}) copy-start(f32[256,512]{1,0:T(8,128)S(1)} %collective-permute-done.8.refs_3_.refs_11_) | copy-start | bytes 1572868

commit v5 on v4

--- a/solution.py
+++ b/solution.py
@@ -26,20 +26,21 @@
     return jnp.dot(left, right, preferred_element_type=jnp.float32)
 
 
-def shape_own(drawn, row_index, col_index, row_count):
+def shape_own(drawn, row_index, first_row, row_count):
     panels, rows, width = drawn.shape
-    local_rows = col_index * rows + jnp.arange(rows, dtype=jnp.int32)
+    local_rows = first_row + jnp.arange(rows, dtype=jnp.int32)
     matrix_rows = local_rows // BLOCK * BLOCK * row_count + row_index * BLOCK + local_rows % BLOCK
     matrix_rows = matrix_rows[None, :, None]
     diagonal_at = (
         jnp.arange(panels, dtype=jnp.int32)[:, None, None] * width
         + jnp.arange(width, dtype=jnp.int32)[None, None, :]
     )
-    return jnp.where(
+    shaped = jnp.where(
         matrix_rows < diagonal_at,
         jnp.float32(0.0),
         jnp.where(matrix_rows == diagonal_at, jnp.float32(1.0), drawn),
     )
+    return jnp.concatenate([shaped[1], shaped[0]], axis=1)
 
 
 def move_x(value, shift):
@@ -154,13 +155,11 @@
 
 
 def times(left, right):
-    return lax.dot_general(
-        left,
-        right,
-        (((1,), (1,)), ((), ())),
-        precision=lax.Precision.HIGHEST,
-        preferred_element_type=jnp.float32,
-    )
+    def part(one, other):
+        return lax.dot_general(one, other, (((1,), (1,)), ((), ())), preferred_element_type=jnp.float32)
+
+    (left_high, left_low), (high, low) = split(left), split(right)
+    return part(left_high, high) + (part(left_high, low) + part(left_low, high))
 
 
 def triangle(tau):
@@ -257,11 +256,12 @@
     )
     eigs = eigvecs.reshape(NY, NX, reflectors.shape[1], eigvecs.shape[1])
 
-    own = shape_own(reflectors, row_index, col_index, row_count)
-    own = jnp.concatenate([own[1], own[0]], axis=1)
-
-    own_a = lax.all_gather(own[:ROWS_A], "col", axis=0, tiled=True, axis_index_groups=GROUPS_X)
-    own_b = spread(own[ROWS_A:], GROUPS_Y).reshape(-1, width)
+    first_row = col_index * reflectors.shape[1]
+    rest = shape_own(reflectors[:, ROWS_A:], row_index, first_row + ROWS_A, row_count)
+    own = shape_own(reflectors[:, :ROWS_A], row_index, first_row, row_count)
+
+    own_a = lax.all_gather(own, "col", axis=0, tiled=True, axis_index_groups=GROUPS_X)
+    own_b = spread(rest, GROUPS_Y).reshape(-1, width)
     own_b, _ = lax.optimization_barrier((own_b, own_a))
     up, down = [own_a], [own_a]
     for _ in range(NY // 2 - 1):

time: 152 us -> 151 us (level)
  no operation moved by 1% of the time
where the time goes in v5:
time: 151 us; the launch traced here: 150 us
  blocking collectives  58.5 us (39%)
  starting transfers between devices  38.9 us (26%)
  waiting for transfers between devices  31.7 us (21%)
  Pallas kernels  18.6 us (12%)
    all_to_all x1, blocking collectives, shards(): share = jnp.sum(lax.all_to_all(shares, 'row', 0, 0), axis=0)  30.4 us
    ppermute x7, starting transfers between devices, move_y(): return lax.ppermute(value, 'col', pairs)  19.7 us
    all_gather x1, blocking collectives, shards(): sums = lax.all_gather(share, 'row')  15.9 us
    ppermute x7, waiting for transfers between devices, move_y(): return lax.ppermute(value, 'col', pairs)  15.5 us
    all_gather x1, blocking collectives, shards(): lax.all_gather(own, 'col', axis=0, tiled=True, axis_index_groups=GROUPS_X)  12.2 us
    ppermute x3, starting transfers between devices, move_x(): return lax.ppermute(value, 'col', pairs)  11.6 us
    all_to_all x1, waiting for transfers between devices, spread(): return lax.all_to_all(copies, 'col', 0, 0, axis_index_groups=groups)  11.6 us
    pallas_call x3, Pallas kernels, inner_products(): pl.pallas_call(functools.partial(inner_kernel, shifts, starts is None, bo...  10.2 us
  transfers between devices with their start and end apart: 11, of which 9 were waited for; matrix products, arithmetic and copies ran while one was open for 0% of the time, Pallas kernels for 5%

profile of v5, /device:TPU:1, one launch (start us, length us, event | category | flops | bytes accessed | tf_op | source)
XLA Modules:
  0.0 150.5 jit_solution(14628064609487347381)
XLA Ops:
  0.0 0.1 iota_add_fusion
  0.1 1.1 select_select_fusion
  1.2 0.0 copy-start.5
  1.3 1.1 broadcast_in_dim.23
  2.4 7.7 %all-to-all-start = ((f32[8,64,512]{2,1,0:T(8,128)}), f32[8,64,512]{2,1,0:T(8,128)S(1)}, u32[]{:S(2)}, u32[]{:S(2)}) async-start(f32[8,64,512]{2,1,0:T(8,128)} %broadcast_in_dim.23), calls=%async_computation | async-start | bytes 2097152 | tf_op jit(solution)/shard_map/all_to_all | solution.py:63
  10.0 12.2 %all_gather.9.refs_1_.refs_4_ = f32[256,512]{1,0:T(8,128)} all-gather(f32[64,512]{1,0:T(8,128)S(1)} %pad_maximum_fusion.1), channel_id=1, replica_groups={{0,1,2,3},{4,5,6,7},{8,9,10,11},{12,13,14,15},{16,17,18,19},{20,21,22,2..., dimensions={0}, use_global_device_ids=true | all-gather | bytes 655360 | tf_op jit(solution)/shard_map/all_gather | solution.py:263
  22.2 3.6 %collective-permute-start.2 = (f32[256,512]{1,0:T(8,128)}, f32[256,512]{1,0:T(8,128)}, u32[]{:S(2)}, u32[]{:S(2)}) collective-permute-start(f32[256,512]{1,0:T(8,128)} %all_gather.9.refs_1_.refs_4_), channel_id=1, source_target_pairs={{0,4},{1,5},{2,6},{3,7},{4,8},{5,9},{6,10},{7,11},{8,12},{9,13},{1... | collective-permute-start | bytes 1572872 | tf_op jit(solution)/shard_map/ppermute | solution.py:53
  25.8 11.6 %all-to-all-done = f32[8,64,512]{2,1,0:T(8,128)S(1)} async-done(((f32[8,64,512]{2,1,0:T(8,128)}), f32[8,64,512]{2,1,0:T(8,128)S(1)}, u32[]{:S(2)}, u32[]{:S(2)}) %all-to-all-start) | async-done | bytes 1048608 | tf_op jit(solution)/shard_map/all_to_all | solution.py:63
  37.4 4.9 %collective-permute-start = (f32[512,512]{1,0:T(8,128)S(1)}, f32[512,512]{1,0:T(8,128)}, u32[]{:S(2)}, u32[]{:S(2)}) collective-permute-start(f32[512,512]{1,0:T(8,128)S(1)} %bitcast.16), channel_id=1, source_target_pairs={{0,1},{1,2},{2,3},{3,0},{4,5},{5,6},{6,7},{7,4},{8,9},{9,10},{10,1... | collective-permute-start | bytes 3145736 | tf_op jit(solution)/shard_map/ppermute | solution.py:48
  42.3 1.9 %collective-permute-start.5 = (f32[256,512]{1,0:T(8,128)}, f32[256,512]{1,0:T(8,128)}, u32[]{:S(2)}, u32[]{:S(2)}) collective-permute-start(f32[256,512]{1,0:T(8,128)} %all_gather.9.refs_1_.refs_4_), channel_id=1, source_target_pairs={{0,28},{1,29},{2,30},{3,31},{4,0},{5,1},{6,2},{7,3},{8,4},{9,5},{1... | collective-permute-start | bytes 1572872 | tf_op jit(solution)/shard_map/ppermute | solution.py:53
  44.2 2.5 %collective-permute-done.2.refs_2_.refs_5_ = f32[256,512]{1,0:T(8,128)} collective-permute-done((f32[256,512]{1,0:T(8,128)}, f32[256,512]{1,0:T(8,128)}, u32[]{:S(2)}, u32[]{:S(2)}) %collective-permute-start.2) | collective-permute-done | bytes 524320 | tf_op jit(solution)/shard_map/ppermute | solution.py:53
  46.8 1.9 %collective-permute-start.3 = (f32[256,512]{1,0:T(8,128)}, f32[256,512]{1,0:T(8,128)}, u32[]{:S(2)}, u32[]{:S(2)}) collective-permute-start(f32[256,512]{1,0:T(8,128)} %collective-permute-done.2.refs_2_.refs_5_), channel_id=1, source_target_pairs={{0,4},{1,5},{2,6},{3,7},{4,8},{5,9},{6,10},{7,11},{8,12},{9,13},{1... | collective-permute-start | bytes 1572872 | tf_op jit(solution)/shard_map/ppermute | solution.py:53
  48.7 4.5 %collective-permute-start.9 = (f32[512,512]{1,0:T(8,128)S(1)}, f32[512,512]{1,0:T(8,128)}, u32[]{:S(2)}, u32[]{:S(2)}) collective-permute-start(f32[512,512]{1,0:T(8,128)S(1)} %bitcast.17), channel_id=1, source_target_pairs={{0,3},{1,0},{2,1},{3,2},{4,7},{5,4},{6,5},{7,6},{8,11},{9,8},{10,9... | collective-permute-start | bytes 3145736 | tf_op jit(solution)/shard_map/ppermute | solution.py:48
  53.2 3.8 %collective-permute-done.5.refs_3_.refs_6_ = f32[256,512]{1,0:T(8,128)} collective-permute-done((f32[256,512]{1,0:T(8,128)}, f32[256,512]{1,0:T(8,128)}, u32[]{:S(2)}, u32[]{:S(2)}) %collective-permute-start.5) | collective-permute-done | bytes 524320 | tf_op jit(solution)/shard_map/ppermute | solution.py:53
  57.0 3.4 %collective-permute-start.6 = (f32[256,512]{1,0:T(8,128)}, f32[256,512]{1,0:T(8,128)}, u32[]{:S(2)}, u32[]{:S(2)}) collective-permute-start(f32[256,512]{1,0:T(8,128)} %collective-permute-done.5.refs_3_.refs_6_), channel_id=1, source_target_pairs={{0,28},{1,29},{2,30},{3,31},{4,0},{5,1},{6,2},{7,3},{8,4},{9,5},{1... | collective-permute-start | bytes 1572872 | tf_op jit(solution)/shard_map/ppermute | solution.py:53
  60.4 1.6 %collective-permute-done.3.refs_2_.refs_7_ = f32[256,512]{1,0:T(8,128)} collective-permute-done((f32[256,512]{1,0:T(8,128)}, f32[256,512]{1,0:T(8,128)}, u32[]{:S(2)}, u32[]{:S(2)}) %collective-permute-start.3) | collective-permute-done | bytes 524320 | tf_op jit(solution)/shard_map/ppermute | solution.py:53
  62.1 1.9 %collective-permute-start.4 = (f32[256,512]{1,0:T(8,128)}, f32[256,512]{1,0:T(8,128)}, u32[]{:S(2)}, u32[]{:S(2)}) collective-permute-start(f32[256,512]{1,0:T(8,128)} %collective-permute-done.3.refs_2_.refs_7_), channel_id=1, source_target_pairs={{0,4},{1,5},{2,6},{3,7},{4,8},{5,9},{6,10},{7,11},{8,12},{9,13},{1... | collective-permute-start | bytes 1572872 | tf_op jit(solution)/shard_map/ppermute | solution.py:53
  64.0 2.1 %collective-permute-done.refs_0_.refs_1_ = f32[512,512]{1,0:T(8,128)} collective-permute-done((f32[512,512]{1,0:T(8,128)S(1)}, f32[512,512]{1,0:T(8,128)}, u32[]{:S(2)}, u32[]{:S(2)}) %collective-permute-start) | collective-permute-done | bytes 1048608 | tf_op jit(solution)/shard_map/ppermute | solution.py:48
  66.1 2.2 %collective-permute-start.1 = (f32[512,512]{1,0:T(8,128)}, f32[512,512]{1,0:T(8,128)}, u32[]{:S(2)}, u32[]{:S(2)}) collective-permute-start(f32[512,512]{1,0:T(8,128)} %collective-permute-done.refs_0_.refs_1_), channel_id=1, source_target_pairs={{0,1},{1,2},{2,3},{3,0},{4,5},{5,6},{6,7},{7,4},{8,9},{9,10},{10,1... | collective-permute-start | bytes 3145736 | tf_op jit(solution)/shard_map/ppermute | solution.py:48
  68.4 2.4 %collective-permute-done.6.refs_3_.refs_8_ = f32[256,512]{1,0:T(8,128)} collective-permute-done((f32[256,512]{1,0:T(8,128)}, f32[256,512]{1,0:T(8,128)}, u32[]{:S(2)}, u32[]{:S(2)}) %collective-permute-start.6) | collective-permute-done | bytes 524320 | tf_op jit(solution)/shard_map/ppermute | solution.py:53
  70.7 5.0 %collective-permute-start.7 = (f32[256,512]{1,0:T(8,128)}, f32[256,512]{1,0:T(8,128)S(1)}, u32[]{:S(2)}, u32[]{:S(2)}) collective-permute-start(f32[256,512]{1,0:T(8,128)} %collective-permute-done.6.refs_3_.refs_8_), channel_id=1, source_target_pairs={{0,28},{1,29},{2,30},{3,31},{4,0},{5,1},{6,2},{7,3},{8,4},{9,5},{1... | collective-permute-start | bytes 1572872 | tf_op jit(solution)/shard_map/ppermute | solution.py:53
  75.7 0.7 collective-permute-done.4.refs_1_.refs_9_
  76.4 1.9 %collective-permute-start.8 = (f32[256,512]{1,0:T(8,128)}, f32[256,512]{1,0:T(8,128)S(1)}, u32[]{:S(2)}, u32[]{:S(2)}) collective-permute-start(f32[256,512]{1,0:T(8,128)} %collective-permute-done.4.refs_1_.refs_9_), channel_id=1, source_target_pairs={{0,4},{1,5},{2,6},{3,7},{4,8},{5,9},{6,10},{7,11},{8,12},{9,13},{1... | collective-permute-start | bytes 1572872 | tf_op jit(solution)/shard_map/ppermute | solution.py:53
  78.4 0.1 pad_add_fusion.at_ref
  78.5 3.1 %shard_map.55 = (f32[128,512]{1,0:T(8,128)S(1)}, f32[256,256]{1,0:T(8,128)S(1)}) custom-call(s32[12]{0:T(128)S(1)} %pad_add_fusion.at_ref, f32[8,4,128,128]{3,2,1,0:T(8,128)S(1)} %bitcast.13, f32[512,512]{1,0:T(8,128)S(1)} %bitcast.18, f32[256,512]{1,0:T(8,128)} %all_gather.9.refs_1_.refs_4_, f32[256,512]{1,0:T(8,128)} %collective-permute-done.2.refs_2_.refs_5_, ...), custom_call_target="tpu_custom_call" | custom-call | flops 1006632960 | bytes 3276800 | tf_op jit(solution)/shard_map/pallas_call | solution.py:140
  81.6 3.8 %shard_map.56 = (f32[128,512]{1,0:T(8,128)S(1)}, f32[256,256]{1,0:T(8,128)S(1)}) custom-call(s32[12]{0:T(128)S(1)} %pad_add_fusion.at_ref, f32[8,4,128,128]{3,2,1,0:T(8,128)S(1)} %bitcast.14, f32[512,512]{1,0:T(8,128)} %collective-permute-done.refs_0_.refs_1_, f32[512,512]{1,0:T(8,128)} %collective-permute-done.9.refs_1_.refs_2_, ...), custom_call_target="tpu_custom_call" | custom-call | flops 1207959552 | bytes 3932160 | tf_op jit(solution)/shard_map/pallas_call | solution.py:140
  85.5 4.4 %collective-permute-done.8.refs_3_.refs_11_ = f32[256,512]{1,0:T(8,128)S(1)} collective-permute-done((f32[256,512]{1,0:T(8,128)}, f32[256,512]{1,0:T(8,128)S(1)}, u32[]{:S(2)}, u32[]{:S(2)}) %collective-permute-start.8) | collective-permute-done | bytes 524320 | tf_op jit(solution)/shard_map/ppermute | solution.py:53
  89.9 2.6 %collective-permute-done.1.refs_0_.refs_3_ = f32[512,512]{1,0:T(8,128)} collective-permute-done((f32[512,512]{1,0:T(8,128)}, f32[512,512]{1,0:T(8,128)}, u32[]{:S(2)}, u32[]{:S(2)}) %collective-permute-start.1) | collective-permute-done | bytes 1048608 | tf_op jit(solution)/shard_map/ppermute | solution.py:48
  92.5 3.2 %shard_map.57 = f32[16,16,512]{2,1,0:T(8,128)S(1)} custom-call(s32[12]{0:T(128)S(1)} %pad_add_fusion.at_ref, f32[8,4,128,128]{3,2,1,0:T(8,128)S(1)} %bitcast.15, f32[512,512]{1,0:T(8,128)} %collective-permute-done.1.refs_0_.refs_3_, f32[256,512]{1,0:T(8,128)} %collective-permute-done.4.refs_1_.refs_9_, ...), custom_call_target="tpu_custom_call" | custom-call | flops 1006632960 | bytes 3276800 | tf_op jit(solution)/shard_map/pallas_call | solution.py:140
  95.7 30.4 %all_to_all.10 = f32[16,16,512]{2,1,0:T(8,128)S(1)} all-to-all(f32[16,16,512]{2,1,0:T(8,128)S(1)} %shard_map.57), channel_id=1, replica_groups=mesh['row'=16,'col'=32] {'row'}, dimensions={0} | all-to-all | bytes 1048576 | tf_op jit(solution)/shard_map/all_to_all | solution.py:279
  126.1 15.9 %all-gather = f32[256,512]{1,0:T(8,128)S(1)} all-gather(f32[16,512]{1,0:T(8,128)S(1)} %reduce_sum.9), channel_id=2, replica_groups=mesh['row'=16,'col'=32] {'row'}, dimensions={0}, use_global_device_ids=true | all-gather | bytes 557056 | tf_op jit(solution)/shard_map/all_gather | solution.py:280
  142.0 8.5 %shard_map.58 = f32[8,4,128,128]{3,2,1,0:T(8,128)} custom-call(s32[12]{0:T(128)S(1)} %pad_add_fusion.at_ref, f32[16,16,512]{2,1,0:T(8,128)S(1)} %bitcast.20, f32[2,256,256]{2,1,0:T(8,128)} %tau_hbm.1, f32[8,4,128,128]{3,2,1,0:T(8,128)} %bitcast.12, f32[512,512]{1,0:T(8,128)} %bitcast.19, f32[512,512]{1,0:T(8,128)} %collective-permute-done.refs_0_.refs_1_, ...), custom_call_target="tpu_custom_call" | custom-call | flops 1610612736 | bytes 12582912 | tf_op jit(solution)/shard_map/pallas_call | solution.py:223
  (22 shorter events, 0.2 us)
Async XLA Ops:
  1.2 67.1 %copy-start.5 = (s32[8]{0:T(128)S(1)}, s32[8]{0:T(128)}, u32[]{:S(2)}) copy-start(s32[8]{0:T(128)} %constant.112.clone) | copy-start | bytes 100
  1.2 77.1 %copy-start.4 = (s32[4]{0:T(128)S(1)}, s32[4]{0:T(128)}, u32[]{:S(2)}) copy-start(s32[4]{0:T(128)} %constant.111.clone) | copy-start | bytes 52
  1.2 77.2 %copy-start = (f32[4096,128]{1,0:T(8,128)S(1)}, f32[4096,128]{1,0:T(8,128)}, u32[]{:S(2)}) copy-start(f32[4096,128]{1,0:T(8,128)} %param.5) | copy-start | bytes 6291460
  2.4 35.1 %all-to-all-start = ((f32[8,64,512]{2,1,0:T(8,128)}), f32[8,64,512]{2,1,0:T(8,128)S(1)}, u32[]{:S(2)}, u32[]{:S(2)}) async-start(f32[8,64,512]{2,1,0:T(8,128)} %broadcast_in_dim.23), calls=%async_computation | async-start | bytes 2097152 | tf_op jit(solution)/shard_map/all_to_all | solution.py:63
  22.2 24.6 %collective-permute-start.2 = (f32[256,512]{1,0:T(8,128)}, f32[256,512]{1,0:T(8,128)}, u32[]{:S(2)}, u32[]{:S(2)}) collective-permute-start(f32[256,512]{1,0:T(8,128)} %all_gather.9.refs_1_.refs_4_), channel_id=1, source_target_pairs={{0,4},{1,5},{2,6},{3,7},{4,8},{5,9},{6,10},{7,11},{8,12},{9,13},{1... | collective-permute-start | bytes 1572872 | tf_op jit(solution)/shard_map/ppermute | solution.py:53
  37.4 44.2 %copy-start.1 = (f32[8,64,512]{2,1,0:T(8,128)}, f32[8,64,512]{2,1,0:T(8,128)S(1)}, u32[]{:S(2)}) copy-start(f32[8,64,512]{2,1,0:T(8,128)S(1)} %all-to-all-done) | copy-start | bytes 3145732
  37.4 28.7 %collective-permute-start = (f32[512,512]{1,0:T(8,128)S(1)}, f32[512,512]{1,0:T(8,128)}, u32[]{:S(2)}, u32[]{:S(2)}) collective-permute-start(f32[512,512]{1,0:T(8,128)S(1)} %bitcast.16), channel_id=1, source_target_pairs={{0,1},{1,2},{2,3},{3,0},{4,5},{5,6},{6,7},{7,4},{8,9},{9,10},{10,1... | collective-permute-start | bytes 3145736 | tf_op jit(solution)/shard_map/ppermute | solution.py:48
  42.3 14.7 %collective-permute-start.5 = (f32[256,512]{1,0:T(8,128)}, f32[256,512]{1,0:T(8,128)}, u32[]{:S(2)}, u32[]{:S(2)}) collective-permute-start(f32[256,512]{1,0:T(8,128)} %all_gather.9.refs_1_.refs_4_), channel_id=1, source_target_pairs={{0,28},{1,29},{2,30},{3,31},{4,0},{5,1},{6,2},{7,3},{8,4},{9,5},{1... | collective-permute-start | bytes 1572872 | tf_op jit(solution)/shard_map/ppermute | solution.py:53
  46.8 15.3 %collective-permute-start.3 = (f32[256,512]{1,0:T(8,128)}, f32[256,512]{1,0:T(8,128)}, u32[]{:S(2)}, u32[]{:S(2)}) collective-permute-start(f32[256,512]{1,0:T(8,128)} %collective-permute-done.2.refs_2_.refs_5_), channel_id=1, source_target_pairs={{0,4},{1,5},{2,6},{3,7},{4,8},{5,9},{6,10},{7,11},{8,12},{9,13},{1... | collective-permute-start | bytes 1572872 | tf_op jit(solution)/shard_map/ppermute | solution.py:53
  48.7 32.9 %collective-permute-start.9 = (f32[512,512]{1,0:T(8,128)S(1)}, f32[512,512]{1,0:T(8,128)}, u32[]{:S(2)}, u32[]{:S(2)}) collective-permute-start(f32[512,512]{1,0:T(8,128)S(1)} %bitcast.17), channel_id=1, source_target_pairs={{0,3},{1,0},{2,1},{3,2},{4,7},{5,4},{6,5},{7,6},{8,11},{9,8},{10,9... | collective-permute-start | bytes 3145736 | tf_op jit(solution)/shard_map/ppermute | solution.py:48
  57.0 13.7 %collective-permute-start.6 = (f32[256,512]{1,0:T(8,128)}, f32[256,512]{1,0:T(8,128)}, u32[]{:S(2)}, u32[]{:S(2)}) collective-permute-start(f32[256,512]{1,0:T(8,128)} %collective-permute-done.5.refs_3_.refs_6_), channel_id=1, source_target_pairs={{0,28},{1,29},{2,30},{3,31},{4,0},{5,1},{6,2},{7,3},{8,4},{9,5},{1... | collective-permute-start | bytes 1572872 | tf_op jit(solution)/shard_map/ppermute | solution.py:53
  62.1 14.4 %collective-permute-start.4 = (f32[256,512]{1,0:T(8,128)}, f32[256,512]{1,0:T(8,128)}, u32[]{:S(2)}, u32[]{:S(2)}) collective-permute-start(f32[256,512]{1,0:T(8,128)} %collective-permute-done.3.refs_2_.refs_7_), channel_id=1, source_target_pairs={{0,4},{1,5},{2,6},{3,7},{4,8},{5,9},{6,10},{7,11},{8,12},{9,13},{1... | collective-permute-start | bytes 1572872 | tf_op jit(solution)/shard_map/ppermute | solution.py:53
  66.1 26.4 %collective-permute-start.1 = (f32[512,512]{1,0:T(8,128)}, f32[512,512]{1,0:T(8,128)}, u32[]{:S(2)}, u32[]{:S(2)}) collective-permute-start(f32[512,512]{1,0:T(8,128)} %collective-permute-done.refs_0_.refs_1_), channel_id=1, source_target_pairs={{0,1},{1,2},{2,3},{3,0},{4,5},{5,6},{6,7},{7,4},{8,9},{9,10},{10,1... | collective-permute-start | bytes 3145736 | tf_op jit(solution)/shard_map/ppermute | solution.py:48
  70.7 14.8 %collective-permute-start.7 = (f32[256,512]{1,0:T(8,128)}, f32[256,512]{1,0:T(8,128)S(1)}, u32[]{:S(2)}, u32[]{:S(2)}) collective-permute-start(f32[256,512]{1,0:T(8,128)} %collective-permute-done.6.refs_3_.refs_8_), channel_id=1, source_target_pairs={{0,28},{1,29},{2,30},{3,31},{4,0},{5,1},{6,2},{7,3},{8,4},{9,5},{1... | collective-permute-start | bytes 1572872 | tf_op jit(solution)/shard_map/ppermute | solution.py:53
  76.4 13.4 %collective-permute-start.8 = (f32[256,512]{1,0:T(8,128)}, f32[256,512]{1,0:T(8,128)S(1)}, u32[]{:S(2)}, u32[]{:S(2)}) collective-permute-start(f32[256,512]{1,0:T(8,128)} %collective-permute-done.4.refs_1_.refs_9_), channel_id=1, source_target_pairs={{0,4},{1,5},{2,6},{3,7},{4,8},{5,9},{6,10},{7,11},{8,12},{9,13},{1... | collective-permute-start | bytes 1572872 | tf_op jit(solution)/shard_map/ppermute | solution.py:53
  85.5 10.1 %copy-start.2 = (f32[256,512]{1,0:T(8,128)}, f32[256,512]{1,0:T(8,128)S(1)}, u32[]{:S(2)}) copy-start(f32[256,512]{1,0:T(8,128)S(1)} %collective-permute-done.7.refs_2_.refs_10_) | copy-start | bytes 1572868
  89.9 5.8 %copy-start.3 = (f32[256,512]{1,0:T(8,128)}, f32[256,512]{1,0:T(8,128)S(1)}, u32[]{:S(2)}) copy-start(f32[256,512]{1,0:T(8,128)S(1)} %collective-permute-done.8.refs_3_.refs_11_) | copy-start | bytes 1572868

commit v6 on v5

--- a/solution.py
+++ b/solution.py
@@ -272,10 +272,10 @@
     far_b = move_x(left, 1)
 
     state = inner_products(at, eigs, ([0], [0, -1, 1]), [own_b, own_a, up[1], down[1]], None, 0)
-    state = inner_products(at, eigs, ([-1, 1], [-2, 2]), [left, right, up[2], down[2]], state, 0)
-    (shares,) = inner_products(
-        at, eigs, ([NX // 2], [-3, 3, NY // 2]), [far_b, up[3], down[3], far_a], state, row_count
-    )
+    state = inner_products(
+        at, eigs, ([-1, 1], [-2, 2, -3, 3]), [left, right, up[2], down[2], up[3], down[3]], state, 0
+    )
+    (shares,) = inner_products(at, eigs, ([NX // 2], [NY // 2]), [far_b, far_a], state, row_count)
     share = jnp.sum(lax.all_to_all(shares, "row", 0, 0), axis=0)
     sums = lax.all_gather(share, "row")
 

time: 151 us -> 151 us (level)
    ppermute x7, waiting for transfers between devices: 15.5 us -> 18.9 us  [move_y(): return lax.ppermute(value, 'col', pairs)]
    ppermute x3, waiting for transfers between devices: 4.67 us -> 1.45 us  [move_x(): return lax.ppermute(value, 'col', pairs)]
  transfers between devices with their start and end apart: 11 -> 11, of which waited for: 9 -> 10; matrix products, arithmetic and copies ran while one was open for 0% -> 0% of each run, Pallas kernels for 5% -> 5%
where the time goes in v6:
time: 151 us
  blocking collectives  59.7 us (40%)
  starting transfers between devices  37.5 us (25%)
  waiting for transfers between devices  32 us (21%)
  Pallas kernels  18.8 us (12%)
    all_to_all x1, blocking collectives, shards(): share = jnp.sum(lax.all_to_all(shares, 'row', 0, 0), axis=0)  31.6 us
    ppermute x7, starting transfers between devices, move_y(): return lax.ppermute(value, 'col', pairs)  19.7 us
    ppermute x7, waiting for transfers between devices, move_y(): return lax.ppermute(value, 'col', pairs)  18.9 us
    all_gather x1, blocking collectives, shards(): sums = lax.all_gather(share, 'row')  15.9 us
    all_gather x1, blocking collectives, shards(): lax.all_gather(own, 'col', axis=0, tiled=True, axis_index_groups=GROUPS_X)  12.2 us
    all_to_all x1, waiting for transfers between devices, spread(): return lax.all_to_all(copies, 'col', 0, 0, axis_index_groups=groups)  11.6 us
    pallas_call x3, Pallas kernels, inner_products(): pl.pallas_call(functools.partial(inner_kernel, shifts, starts is None, bo...  10.3 us
    ppermute x3, starting transfers between devices, move_x(): return lax.ppermute(value, 'col', pairs)  10.2 us
  transfers between devices with their start and end apart: 11, of which 10 were waited for; matrix products, arithmetic and copies ran while one was open for 0% of the time, Pallas kernels for 5%

profile of v6, /device:TPU:1, one launch (start us, length us, event | category | flops | bytes accessed | tf_op | source)
XLA Modules:
  0.0 150.7 jit_solution(10536725428585542564)
XLA Ops:
  0.0 0.1 iota_add_fusion
  0.1 1.1 select_select_fusion
  1.3 1.1 broadcast_in_dim.23
  2.4 7.7 %all-to-all-start = ((f32[8,64,512]{2,1,0:T(8,128)}), f32[8,64,512]{2,1,0:T(8,128)S(1)}, u32[]{:S(2)}, u32[]{:S(2)}) async-start(f32[8,64,512]{2,1,0:T(8,128)} %broadcast_in_dim.23), calls=%async_computation | async-start | bytes 2097152 | tf_op jit(solution)/shard_map/all_to_all | solution.py:63
  10.0 12.2 %all_gather.9.refs_1_.refs_4_ = f32[256,512]{1,0:T(8,128)} all-gather(f32[64,512]{1,0:T(8,128)S(1)} %pad_maximum_fusion.1), channel_id=1, replica_groups={{0,1,2,3},{4,5,6,7},{8,9,10,11},{12,13,14,15},{16,17,18,19},{20,21,22,2..., dimensions={0}, use_global_device_ids=true | all-gather | bytes 655360 | tf_op jit(solution)/shard_map/all_gather | solution.py:263
  22.2 3.6 %collective-permute-start.2 = (f32[256,512]{1,0:T(8,128)}, f32[256,512]{1,0:T(8,128)}, u32[]{:S(2)}, u32[]{:S(2)}) collective-permute-start(f32[256,512]{1,0:T(8,128)} %all_gather.9.refs_1_.refs_4_), channel_id=1, source_target_pairs={{0,4},{1,5},{2,6},{3,7},{4,8},{5,9},{6,10},{7,11},{8,12},{9,13},{1... | collective-permute-start | bytes 1572872 | tf_op jit(solution)/shard_map/ppermute | solution.py:53
  25.8 11.6 %all-to-all-done = f32[8,64,512]{2,1,0:T(8,128)S(1)} async-done(((f32[8,64,512]{2,1,0:T(8,128)}), f32[8,64,512]{2,1,0:T(8,128)S(1)}, u32[]{:S(2)}, u32[]{:S(2)}) %all-to-all-start) | async-done | bytes 1048608 | tf_op jit(solution)/shard_map/all_to_all | solution.py:63
  37.4 4.9 %collective-permute-start = (f32[512,512]{1,0:T(8,128)S(1)}, f32[512,512]{1,0:T(8,128)}, u32[]{:S(2)}, u32[]{:S(2)}) collective-permute-start(f32[512,512]{1,0:T(8,128)S(1)} %bitcast.16), channel_id=1, source_target_pairs={{0,1},{1,2},{2,3},{3,0},{4,5},{5,6},{6,7},{7,4},{8,9},{9,10},{10,1... | collective-permute-start | bytes 3145736 | tf_op jit(solution)/shard_map/ppermute | solution.py:48
  42.3 1.9 %collective-permute-start.7 = (f32[256,512]{1,0:T(8,128)}, f32[256,512]{1,0:T(8,128)}, u32[]{:S(2)}, u32[]{:S(2)}) collective-permute-start(f32[256,512]{1,0:T(8,128)} %all_gather.9.refs_1_.refs_4_), channel_id=1, source_target_pairs={{0,28},{1,29},{2,30},{3,31},{4,0},{5,1},{6,2},{7,3},{8,4},{9,5},{1... | collective-permute-start | bytes 1572872 | tf_op jit(solution)/shard_map/ppermute | solution.py:53
  44.2 2.5 %collective-permute-done.2.refs_2_.refs_5_ = f32[256,512]{1,0:T(8,128)} collective-permute-done((f32[256,512]{1,0:T(8,128)}, f32[256,512]{1,0:T(8,128)}, u32[]{:S(2)}, u32[]{:S(2)}) %collective-permute-start.2) | collective-permute-done | bytes 524320 | tf_op jit(solution)/shard_map/ppermute | solution.py:53
  46.8 1.9 %collective-permute-start.3 = (f32[256,512]{1,0:T(8,128)}, f32[256,512]{1,0:T(8,128)}, u32[]{:S(2)}, u32[]{:S(2)}) collective-permute-start(f32[256,512]{1,0:T(8,128)} %collective-permute-done.2.refs_2_.refs_5_), channel_id=1, source_target_pairs={{0,4},{1,5},{2,6},{3,7},{4,8},{5,9},{6,10},{7,11},{8,12},{9,13},{1... | collective-permute-start | bytes 1572872 | tf_op jit(solution)/shard_map/ppermute | solution.py:53
  48.7 8.3 %collective-permute-done.7.refs_3_.refs_6_ = f32[256,512]{1,0:T(8,128)} collective-permute-done((f32[256,512]{1,0:T(8,128)}, f32[256,512]{1,0:T(8,128)}, u32[]{:S(2)}, u32[]{:S(2)}) %collective-permute-start.7) | collective-permute-done | bytes 524320 | tf_op jit(solution)/shard_map/ppermute | solution.py:53
  57.0 3.4 %collective-permute-start.8 = (f32[256,512]{1,0:T(8,128)}, f32[256,512]{1,0:T(8,128)}, u32[]{:S(2)}, u32[]{:S(2)}) collective-permute-start(f32[256,512]{1,0:T(8,128)} %collective-permute-done.7.refs_3_.refs_6_), channel_id=1, source_target_pairs={{0,28},{1,29},{2,30},{3,31},{4,0},{5,1},{6,2},{7,3},{8,4},{9,5},{1... | collective-permute-start | bytes 1572872 | tf_op jit(solution)/shard_map/ppermute | solution.py:53
  60.4 3.1 %collective-permute-start.6 = (f32[512,512]{1,0:T(8,128)S(1)}, f32[512,512]{1,0:T(8,128)}, u32[]{:S(2)}, u32[]{:S(2)}) collective-permute-start(f32[512,512]{1,0:T(8,128)S(1)} %bitcast.17), channel_id=1, source_target_pairs={{0,3},{1,0},{2,1},{3,2},{4,7},{5,4},{6,5},{7,6},{8,11},{9,8},{10,9... | collective-permute-start | bytes 3145736 | tf_op jit(solution)/shard_map/ppermute | solution.py:48
  63.5 1.9 %collective-permute-start.4 = (f32[256,512]{1,0:T(8,128)}, f32[256,512]{1,0:T(8,128)}, u32[]{:S(2)}, u32[]{:S(2)}) collective-permute-start(f32[256,512]{1,0:T(8,128)} %collective-permute-done.3.refs_2_.refs_7_), channel_id=1, source_target_pairs={{0,4},{1,5},{2,6},{3,7},{4,8},{5,9},{6,10},{7,11},{8,12},{9,13},{1... | collective-permute-start | bytes 1572872 | tf_op jit(solution)/shard_map/ppermute | solution.py:53
  65.4 0.7 collective-permute-done.refs_0_.refs_1_
  66.1 2.2 %collective-permute-start.1 = (f32[512,512]{1,0:T(8,128)}, f32[512,512]{1,0:T(8,128)}, u32[]{:S(2)}, u32[]{:S(2)}) collective-permute-start(f32[512,512]{1,0:T(8,128)} %collective-permute-done.refs_0_.refs_1_), channel_id=1, source_target_pairs={{0,1},{1,2},{2,3},{3,0},{4,5},{5,6},{6,7},{7,4},{8,9},{9,10},{10,1... | collective-permute-start | bytes 3145736 | tf_op jit(solution)/shard_map/ppermute | solution.py:48
  68.3 2.4 %collective-permute-done.8.refs_3_.refs_8_ = f32[256,512]{1,0:T(8,128)} collective-permute-done((f32[256,512]{1,0:T(8,128)}, f32[256,512]{1,0:T(8,128)}, u32[]{:S(2)}, u32[]{:S(2)}) %collective-permute-start.8) | collective-permute-done | bytes 524320 | tf_op jit(solution)/shard_map/ppermute | solution.py:53
  70.7 5.0 %collective-permute-start.9 = (f32[256,512]{1,0:T(8,128)}, f32[256,512]{1,0:T(8,128)}, u32[]{:S(2)}, u32[]{:S(2)}) collective-permute-start(f32[256,512]{1,0:T(8,128)} %collective-permute-done.8.refs_3_.refs_8_), channel_id=1, source_target_pairs={{0,28},{1,29},{2,30},{3,31},{4,0},{5,1},{6,2},{7,3},{8,4},{9,5},{1... | collective-permute-start | bytes 1572872 | tf_op jit(solution)/shard_map/ppermute | solution.py:53
  75.7 2.3 %collective-permute-done.4.refs_4_.refs_9_ = f32[256,512]{1,0:T(8,128)} collective-permute-done((f32[256,512]{1,0:T(8,128)}, f32[256,512]{1,0:T(8,128)}, u32[]{:S(2)}, u32[]{:S(2)}) %collective-permute-start.4) | collective-permute-done | bytes 524320 | tf_op jit(solution)/shard_map/ppermute | solution.py:53
  78.1 1.9 %collective-permute-start.5 = (f32[256,512]{1,0:T(8,128)}, f32[256,512]{1,0:T(8,128)S(1)}, u32[]{:S(2)}, u32[]{:S(2)}) collective-permute-start(f32[256,512]{1,0:T(8,128)} %collective-permute-done.4.refs_4_.refs_9_), channel_id=1, source_target_pairs={{0,4},{1,5},{2,6},{3,7},{4,8},{5,9},{6,10},{7,11},{8,12},{9,13},{1... | collective-permute-start | bytes 1572872 | tf_op jit(solution)/shard_map/ppermute | solution.py:53
  80.0 0.1 pad_add_fusion.at_ref
  80.1 3.1 %shard_map.55 = (f32[128,512]{1,0:T(8,128)S(1)}, f32[256,256]{1,0:T(8,128)S(1)}) custom-call(s32[12]{0:T(128)S(1)} %pad_add_fusion.at_ref, f32[8,4,128,128]{3,2,1,0:T(8,128)S(1)} %bitcast.13, f32[512,512]{1,0:T(8,128)S(1)} %bitcast.18, f32[256,512]{1,0:T(8,128)} %all_gather.9.refs_1_.refs_4_, f32[256,512]{1,0:T(8,128)} %collective-permute-done.2.refs_2_.refs_5_, ...), custom_call_target="tpu_custom_call" | custom-call | flops 1006632960 | bytes 3276800 | tf_op jit(solution)/shard_map/pallas_call | solution.py:140
  83.3 1.5 collective-permute-done.9.refs_5_.refs_10_
  84.7 0.5 collective-permute-done.6.refs_1_.refs_2_
  85.3 4.6 %shard_map.56 = (f32[128,512]{1,0:T(8,128)S(1)}, f32[256,256]{1,0:T(8,128)S(1)}) custom-call(s32[12]{0:T(128)S(1)} %pad_add_fusion.at_ref, f32[8,4,128,128]{3,2,1,0:T(8,128)S(1)} %bitcast.14, f32[512,512]{1,0:T(8,128)} %collective-permute-done.refs_0_.refs_1_, f32[512,512]{1,0:T(8,128)} %collective-permute-done.6.refs_1_.refs_2_, ...), custom_call_target="tpu_custom_call" | custom-call | flops 1610612736 | bytes 5242880 | tf_op jit(solution)/shard_map/pallas_call | solution.py:140
  89.8 1.9 %collective-permute-done.5.refs_1_.refs_11_ = f32[256,512]{1,0:T(8,128)S(1)} collective-permute-done((f32[256,512]{1,0:T(8,128)}, f32[256,512]{1,0:T(8,128)S(1)}, u32[]{:S(2)}, u32[]{:S(2)}) %collective-permute-start.5) | collective-permute-done | bytes 524320 | tf_op jit(solution)/shard_map/ppermute | solution.py:53
  91.7 0.3 collective-permute-done.1.refs_0_.refs_3_
  92.0 2.6 %shard_map.57 = f32[16,16,512]{2,1,0:T(8,128)S(1)} custom-call(s32[12]{0:T(128)S(1)} %pad_add_fusion.at_ref, f32[8,4,128,128]{3,2,1,0:T(8,128)S(1)} %bitcast.15, f32[512,512]{1,0:T(8,128)} %collective-permute-done.1.refs_0_.refs_3_, f32[256,512]{1,0:T(8,128)S(1)} %collective-permute-done.5.refs_1_.refs_11_, f32[128,512]{1,0:T(8,128)S(1)} %get-tuple-element.13.refs_2_, ...), custom_call_target="tpu_custom_call" | custom-call | flops 603979776 | bytes 1966080 | tf_op jit(solution)/shard_map/pallas_call | solution.py:140
  94.7 31.6 %all_to_all.10 = f32[16,16,512]{2,1,0:T(8,128)S(1)} all-to-all(f32[16,16,512]{2,1,0:T(8,128)S(1)} %shard_map.57), channel_id=1, replica_groups=mesh['row'=16,'col'=32] {'row'}, dimensions={0} | all-to-all | bytes 1048576 | tf_op jit(solution)/shard_map/all_to_all | solution.py:279
  126.3 15.9 %all-gather = f32[256,512]{1,0:T(8,128)S(1)} all-gather(f32[16,512]{1,0:T(8,128)S(1)} %reduce_sum.9), channel_id=2, replica_groups=mesh['row'=16,'col'=32] {'row'}, dimensions={0}, use_global_device_ids=true | all-gather | bytes 557056 | tf_op jit(solution)/shard_map/all_gather | solution.py:280
  142.2 8.5 %shard_map.58 = f32[8,4,128,128]{3,2,1,0:T(8,128)} custom-call(s32[12]{0:T(128)S(1)} %pad_add_fusion.at_ref, f32[16,16,512]{2,1,0:T(8,128)S(1)} %bitcast.20, f32[2,256,256]{2,1,0:T(8,128)} %tau_hbm.1, f32[8,4,128,128]{3,2,1,0:T(8,128)} %bitcast.12, f32[512,512]{1,0:T(8,128)} %bitcast.19, f32[512,512]{1,0:T(8,128)} %collective-permute-done.refs_0_.refs_1_, ...), custom_call_target="tpu_custom_call" | custom-call | flops 1610612736 | bytes 12582912 | tf_op jit(solution)/shard_map/pallas_call | solution.py:223
  (20 shorter events, 0.1 us)
Async XLA Ops:
  1.2 74.5 %copy-start.4 = (s32[8]{0:T(128)S(1)}, s32[8]{0:T(128)}, u32[]{:S(2)}) copy-start(s32[8]{0:T(128)} %constant.112.clone) | copy-start | bytes 100
  1.2 78.8 %copy-start.3 = (s32[4]{0:T(128)S(1)}, s32[4]{0:T(128)}, u32[]{:S(2)}) copy-start(s32[4]{0:T(128)} %constant.111.clone) | copy-start | bytes 52
  1.2 78.9 %copy-start = (f32[4096,128]{1,0:T(8,128)S(1)}, f32[4096,128]{1,0:T(8,128)}, u32[]{:S(2)}) copy-start(f32[4096,128]{1,0:T(8,128)} %param.5) | copy-start | bytes 6291460
  2.4 35.1 %all-to-all-start = ((f32[8,64,512]{2,1,0:T(8,128)}), f32[8,64,512]{2,1,0:T(8,128)S(1)}, u32[]{:S(2)}, u32[]{:S(2)}) async-start(f32[8,64,512]{2,1,0:T(8,128)} %broadcast_in_dim.23), calls=%async_computation | async-start | bytes 2097152 | tf_op jit(solution)/shard_map/all_to_all | solution.py:63
  22.2 24.6 %collective-permute-start.2 = (f32[256,512]{1,0:T(8,128)}, f32[256,512]{1,0:T(8,128)}, u32[]{:S(2)}, u32[]{:S(2)}) collective-permute-start(f32[256,512]{1,0:T(8,128)} %all_gather.9.refs_1_.refs_4_), channel_id=1, source_target_pairs={{0,4},{1,5},{2,6},{3,7},{4,8},{5,9},{6,10},{7,11},{8,12},{9,13},{1... | collective-permute-start | bytes 1572872 | tf_op jit(solution)/shard_map/ppermute | solution.py:53
  37.4 45.9 %copy-start.1 = (f32[8,64,512]{2,1,0:T(8,128)}, f32[8,64,512]{2,1,0:T(8,128)S(1)}, u32[]{:S(2)}) copy-start(f32[8,64,512]{2,1,0:T(8,128)S(1)} %all-to-all-done) | copy-start | bytes 3145732
  37.4 28.7 %collective-permute-start = (f32[512,512]{1,0:T(8,128)S(1)}, f32[512,512]{1,0:T(8,128)}, u32[]{:S(2)}, u32[]{:S(2)}) collective-permute-start(f32[512,512]{1,0:T(8,128)S(1)} %bitcast.16), channel_id=1, source_target_pairs={{0,1},{1,2},{2,3},{3,0},{4,5},{5,6},{6,7},{7,4},{8,9},{9,10},{10,1... | collective-permute-start | bytes 3145736 | tf_op jit(solution)/shard_map/ppermute | solution.py:48
  42.3 14.7 %collective-permute-start.7 = (f32[256,512]{1,0:T(8,128)}, f32[256,512]{1,0:T(8,128)}, u32[]{:S(2)}, u32[]{:S(2)}) collective-permute-start(f32[256,512]{1,0:T(8,128)} %all_gather.9.refs_1_.refs_4_), channel_id=1, source_target_pairs={{0,28},{1,29},{2,30},{3,31},{4,0},{5,1},{6,2},{7,3},{8,4},{9,5},{1... | collective-permute-start | bytes 1572872 | tf_op jit(solution)/shard_map/ppermute | solution.py:53
  46.8 16.7 %collective-permute-start.3 = (f32[256,512]{1,0:T(8,128)}, f32[256,512]{1,0:T(8,128)}, u32[]{:S(2)}, u32[]{:S(2)}) collective-permute-start(f32[256,512]{1,0:T(8,128)} %collective-permute-done.2.refs_2_.refs_5_), channel_id=1, source_target_pairs={{0,4},{1,5},{2,6},{3,7},{4,8},{5,9},{6,10},{7,11},{8,12},{9,13},{1... | collective-permute-start | bytes 1572872 | tf_op jit(solution)/shard_map/ppermute | solution.py:53
  57.0 13.7 %collective-permute-start.8 = (f32[256,512]{1,0:T(8,128)}, f32[256,512]{1,0:T(8,128)}, u32[]{:S(2)}, u32[]{:S(2)}) collective-permute-start(f32[256,512]{1,0:T(8,128)} %collective-permute-done.7.refs_3_.refs_6_), channel_id=1, source_target_pairs={{0,28},{1,29},{2,30},{3,31},{4,0},{5,1},{6,2},{7,3},{8,4},{9,5},{1... | collective-permute-start | bytes 1572872 | tf_op jit(solution)/shard_map/ppermute | solution.py:53
  60.4 24.8 %collective-permute-start.6 = (f32[512,512]{1,0:T(8,128)S(1)}, f32[512,512]{1,0:T(8,128)}, u32[]{:S(2)}, u32[]{:S(2)}) collective-permute-start(f32[512,512]{1,0:T(8,128)S(1)} %bitcast.17), channel_id=1, source_target_pairs={{0,3},{1,0},{2,1},{3,2},{4,7},{5,4},{6,5},{7,6},{8,11},{9,8},{10,9... | collective-permute-start | bytes 3145736 | tf_op jit(solution)/shard_map/ppermute | solution.py:48
  63.5 14.6 %collective-permute-start.4 = (f32[256,512]{1,0:T(8,128)}, f32[256,512]{1,0:T(8,128)}, u32[]{:S(2)}, u32[]{:S(2)}) collective-permute-start(f32[256,512]{1,0:T(8,128)} %collective-permute-done.3.refs_2_.refs_7_), channel_id=1, source_target_pairs={{0,4},{1,5},{2,6},{3,7},{4,8},{5,9},{6,10},{7,11},{8,12},{9,13},{1... | collective-permute-start | bytes 1572872 | tf_op jit(solution)/shard_map/ppermute | solution.py:53
  66.1 25.9 %collective-permute-start.1 = (f32[512,512]{1,0:T(8,128)}, f32[512,512]{1,0:T(8,128)}, u32[]{:S(2)}, u32[]{:S(2)}) collective-permute-start(f32[512,512]{1,0:T(8,128)} %collective-permute-done.refs_0_.refs_1_), channel_id=1, source_target_pairs={{0,1},{1,2},{2,3},{3,0},{4,5},{5,6},{6,7},{7,4},{8,9},{9,10},{10,1... | collective-permute-start | bytes 3145736 | tf_op jit(solution)/shard_map/ppermute | solution.py:48
  70.7 14.0 %collective-permute-start.9 = (f32[256,512]{1,0:T(8,128)}, f32[256,512]{1,0:T(8,128)}, u32[]{:S(2)}, u32[]{:S(2)}) collective-permute-start(f32[256,512]{1,0:T(8,128)} %collective-permute-done.8.refs_3_.refs_8_), channel_id=1, source_target_pairs={{0,28},{1,29},{2,30},{3,31},{4,0},{5,1},{6,2},{7,3},{8,4},{9,5},{1... | collective-permute-start | bytes 1572872 | tf_op jit(solution)/shard_map/ppermute | solution.py:53
  78.1 13.6 %collective-permute-start.5 = (f32[256,512]{1,0:T(8,128)}, f32[256,512]{1,0:T(8,128)S(1)}, u32[]{:S(2)}, u32[]{:S(2)}) collective-permute-start(f32[256,512]{1,0:T(8,128)} %collective-permute-done.4.refs_4_.refs_9_), channel_id=1, source_target_pairs={{0,4},{1,5},{2,6},{3,7},{4,8},{5,9},{6,10},{7,11},{8,12},{9,13},{1... | collective-permute-start | bytes 1572872 | tf_op jit(solution)/shard_map/ppermute | solution.py:53
  91.7 2.9 %copy-start.2 = (f32[256,512]{1,0:T(8,128)}, f32[256,512]{1,0:T(8,128)S(1)}, u32[]{:S(2)}) copy-start(f32[256,512]{1,0:T(8,128)S(1)} %collective-permute-done.5.refs_1_.refs_11_) | copy-start | bytes 1572868
